TPU v7x, 32 devices: a whole 2x2x4 slice. The times are simulated.
32 devices in a mesh: dom: 16 (over z, y, x), col: 2 (over core).
Axes of the slice: x: 2, y: 2, z: 4, core: 2. Of those that a mesh axis runs over, the one named last changes fastest.
Arguments:
- adjoint_rhs: bfloat16 [3072, 105, 64], P('dom', None, 'col')
- element_blocks: bfloat16 [1536, 420, 420], P('dom', 'col')
- element_faces: int32 [1536, 4], P('dom'), may hold values from 0 to 239, as said below
- send_faces: int32 [16, 48], P('dom'), may hold values from 0 to 191
Outputs:
- second_basis: bfloat16 [3072, 105, 64], P('dom', None, 'col')
- next_vector: bfloat16 [3072, 105, 64], P('dom', None, 'col')
- hessenberg: float32 [5, 64], P(None, 'col')
Inputs may be any that keep to these rules, and one draw needn't show every extreme that they name: `element_faces`: row d * 96 + e belongs to partition d. An entry below 192 is an owned face; an entry 192 + p * 3 + s stands for the face that partition p lists in send_faces at position d * 3 + s. No partition names one of its slots at or above 192 twice, and none names its own index p = d.
All inputs are finite; a program needn't handle non-finite values.
Results may differ from a plain program's by a relative error of at most 0.02.
Values may be sent and summed in bfloat16 or wider, within the bound.
No kernel may reach another device: no remote copies, remote signals or barrier semaphores. Data moves between devices by JAX's collectives and lax.ppermute only.
A program may use at most 192 MiB of HBM per device.

v0:
```python
import jax
import jax.numpy as jnp
from jax import lax
from jax.sharding import PartitionSpec as P

P_SIZE = 105


epsilon = 1e-06


def body(adjoint_rhs, element_blocks, element_faces, send_faces):
    owned_count = adjoint_rhs.shape[0]
    dom_ranks = lax.axis_size("dom")
    entries = float(dom_ranks * owned_count * P_SIZE)
    outgoing_faces = send_faces[0]
    ghost_count = outgoing_faces.shape[0]
    slot_share = element_blocks.shape[1] // P_SIZE
    slot_total = element_blocks.shape[2] // P_SIZE
    element_count = element_blocks.shape[0]
    first_slot = lax.axis_index("col") * slot_share
    chosen_slots = lax.dynamic_slice_in_dim(element_faces, first_slot, slot_share, 1)
    all_slots = element_faces.reshape(-1)

    def transposed(vector_half):
        incoming = lax.all_to_all(
            vector_half[outgoing_faces], "dom", split_axis=0, concat_axis=0, tiled=True
        )
        known_traces = lax.all_gather(
            jnp.concatenate([vector_half, incoming], axis=0), "col", axis=2, tiled=True
        )
        picked = known_traces[chosen_slots].reshape(
            element_count, slot_share * P_SIZE, known_traces.shape[2]
        )
        partial_terms = jnp.einsum(
            "ekb,ekr->ebr", element_blocks, picked, preferred_element_type=jnp.float32
        )
        summed = jax.ops.segment_sum(
            partial_terms.reshape(element_count * slot_total, P_SIZE, known_traces.shape[2]),
            all_slots,
            num_segments=owned_count + ghost_count,
        )
        reduced = lax.psum_scatter(
            summed.astype(jnp.bfloat16), "col", scatter_dimension=2, tiled=True
        ).astype(jnp.float32)
        returned = lax.all_to_all(
            reduced[owned_count:].astype(jnp.bfloat16),
            "dom",
            split_axis=0,
            concat_axis=0,
            tiled=True,
        ).astype(jnp.float32)
        return reduced[:owned_count] + jax.ops.segment_sum(
            returned, outgoing_faces, num_segments=owned_count
        )

    residual = adjoint_rhs.astype(jnp.float32)
    start_norm = jnp.sqrt(
        lax.psum(jnp.sum(residual * residual, axis=(0, 1)), "dom") / entries + epsilon
    )
    first_basis = (residual / start_norm).astype(jnp.bfloat16)
    first_image = transposed(first_basis)
    first_float = first_basis.astype(jnp.float32)
    diagonal_term = lax.psum(jnp.sum(first_float * first_image, axis=(0, 1)), "dom") / entries
    projected = first_image - diagonal_term * first_float
    next_norm = jnp.sqrt(
        lax.psum(jnp.sum(projected * projected, axis=(0, 1)), "dom") / entries + epsilon
    )
    second_basis = (projected / next_norm).astype(jnp.bfloat16)
    second_image = transposed(second_basis)
    second_float = second_basis.astype(jnp.float32)
    first_total, second_total = lax.psum(
        (
            jnp.sum(first_float * second_image, axis=(0, 1)),
            jnp.sum(second_float * second_image, axis=(0, 1)),
        ),
        "dom",
    )
    proj_first = first_total / entries
    proj_second = second_total / entries
    next_vector = (second_image - proj_first * first_float - proj_second * second_float).astype(
        jnp.bfloat16
    )
    hessenberg = jnp.stack([start_norm, diagonal_term, next_norm, proj_first, proj_second])
    return (second_basis, next_vector, hessenberg)


def solution(mesh):
    in_specs = (P("dom", None, "col"), P("dom", "col", None), P("dom", None), P("dom", None))
    out_specs = (P("dom", None, "col"), P("dom", None, "col"), P(None, "col"))
    return jax.shard_map(body, mesh=mesh, in_specs=in_specs, out_specs=out_specs, check_vma=False)
```

profile of v0, /device:TPU:0, one launch (start us, length us, event | category | flops | bytes accessed | tf_op | source)
XLA Modules:
  0.0 637.1 jit_solution(9899570503700758773)
XLA Ops:
  9.2 43.5 %psum.35 = f32[32]{0:T(128)S(1)} all-reduce(f32[32]{0:T(128)S(1)} %fusion), channel_id=1, replica_groups=mesh['dom'=16,'col'=2] {'dom'}, use_global_device_ids=true, to_apply=%region_1.0 | all-reduce | flops 32 | bytes 256 | tf_op jit(solution)/shard_map/psum | solution.py:59
  55.7 12.2 %all_to_all.20 = bf16[48,105,32]{1,2,0:T(8,128)(2,1)S(1)} all-to-all(bf16[48,105,32]{1,2,0:T(8,128)(2,1)S(1)} %gather_fusion), channel_id=1, replica_groups=mesh['dom'=16,'col'=2] {'dom'}, dimensions={0} | all-to-all | bytes 645120 | tf_op jit(solution)/shard_map/all_to_all | solution.py:26
  70.1 31.9 %copy.13 = bf16[96,210,420]{1,2,0:T(8,128)(2,1)} copy(bf16[96,210,420]{2,0,1:T(8,128)(2,1)} %param.5) | data formatting | bytes 33868800 | tf_op args[1]
  109.1 4.4 reshape.51
  113.5 12.9 %convolution_bitcast_fusion.1 = f32[96,420,64]{1,2,0:T(8,128)} fusion(bf16[96,210,420]{1,2,0:T(8,128)(2,1)} %copy.13, bf16[96,210,64]{1,0,2:T(8,128)(2,1)S(1)} %reshape.51), kind=kOutput, calls=%fused_computation.13 | convolution fusion | flops 1083801600 | bytes 29836800 | tf_op jit(solution)/shard_map/ekb,ekr->ebr/dot_general | solution.py:35
  126.4 16.3 %copy.14 = f32[96,420,64]{1,0,2:T(8,128)} copy(f32[96,420,64]{1,2,0:T(8,128)} %convolution_bitcast_fusion.1) | data formatting | bytes 20643840 | tf_op jit(solution)/shard_map/ekb,ekr->ebr/dot_general | solution.py:35
  142.7 14.8 %reshape.91 = f32[384,105,64]{1,0,2:T(8,128)} reshape(f32[96,420,64]{1,0,2:T(8,128)} %copy.14) | data formatting | bytes 20643840 | tf_op jit(solution)/shard_map/reshape | solution.py:39
  157.5 16.3 %copy.15 = f32[384,105,64]{1,2,0:T(8,128)} copy(f32[384,105,64]{1,0,2:T(8,128)} %reshape.91) | data formatting | bytes 20643840 | tf_op jit(solution)/shard_map/reshape | solution.py:39
  177.9 59.4 %scatter_fusion = f32[240,105,64]{1,2,0:T(8,128)} fusion(f32[240,105,64]{1,2,0:T(8,128)} %broadcast.46.clone, s32[384]{0:T(512)S(1)} %reshape.89, f32[384,105,64]{1,2,0:T(8,128)} %copy.15), kind=kCustom, calls=%fused_computation.4 | custom fusion | flops 2580480 | bytes 30967296 | tf_op jit(solution)/shard_map/scatter-add | solution.py:38
  237.3 6.1 convert_element_type.36
  243.5 10.9 %reduce-scatter.3.cloned.1.call-done = bf16[240,105,32]{1,2,0:T(8,128)(2,1)} async-done(((bf16[240,105,64]{1,2,0:T(8,128)(2,1)}), bf16[240,105,32]{1,2,0:T(8,128)(2,1)}) %reduce-scatter.3.cloned.1.call-update) | async-done | bytes 1612816 | tf_op jit(solution)/shard_map/reduce_scatter | solution.py:43
  256.2 6.8 %all-to-all-start.1 = ((bf16[48,105,32]{1,2,0:T(8,128)(2,1)}), bf16[48,105,32]{1,2,0:T(8,128)(2,1)S(1)}, u32[]{:S(2)}, u32[]{:S(2)}) async-start(bf16[48,105,32]{1,2,0:T(8,128)(2,1)} %slice.35), calls=%async_computation.2 | async-start | bytes 786432 | tf_op jit(solution)/shard_map/all_to_all | solution.py:46
  266.5 9.5 %all-to-all-done.1 = bf16[48,105,32]{1,2,0:T(8,128)(2,1)S(1)} async-done(((bf16[48,105,32]{1,2,0:T(8,128)(2,1)}), bf16[48,105,32]{1,2,0:T(8,128)(2,1)S(1)}, u32[]{:S(2)}, u32[]{:S(2)}) %all-to-all-start.1) | async-done | bytes 322592 | tf_op jit(solution)/shard_map/all_to_all | solution.py:46
  276.1 6.2 scatter_fusion.1
  285.0 39.0 %psum.36 = f32[32]{0:T(128)S(1)} all-reduce(f32[32]{0:T(128)S(1)} %fusion.5), channel_id=1, replica_groups=mesh['dom'=16,'col'=2] {'dom'}, use_global_device_ids=true, to_apply=%region_6.0 | all-reduce | flops 32 | bytes 256 | tf_op jit(solution)/shard_map/psum | solution.py:64
  327.2 36.7 %psum.37 = f32[32]{0:T(128)S(1)} all-reduce(f32[32]{0:T(128)S(1)} %multiply_reduce_fusion), channel_id=1, replica_groups=mesh['dom'=16,'col'=2] {'dom'}, use_global_device_ids=true, to_apply=%region_8.0 | all-reduce | flops 32 | bytes 256 | tf_op jit(solution)/shard_map/psum | solution.py:67
  367.6 12.9 %all_to_all.21 = bf16[48,105,32]{1,2,0:T(8,128)(2,1)S(1)} all-to-all(bf16[48,105,32]{1,2,0:T(8,128)(2,1)S(1)} %gather_fusion.2), channel_id=1, replica_groups=mesh['dom'=16,'col'=2] {'dom'}, dimensions={0} | all-to-all | bytes 645120 | tf_op jit(solution)/shard_map/all_to_all | solution.py:26
  382.3 11.6 %all-gather.5.cloned.1.call-done = bf16[240,105,64]{1,2,0:T(8,128)(2,1)} async-done(((bf16[240,105,32]{1,2,0:T(8,128)(2,1)}), bf16[240,105,64]{1,2,0:T(8,128)(2,1)}) %all-gather.5.cloned.1.call-update) | async-done | bytes 3225616 | tf_op jit(solution)/shard_map/all_gather | solution.py:29
  393.9 4.9 gather_fusion.3
  398.8 5.6 copy.16
  404.4 5.9 reshape.53
  410.3 13.6 %convolution_bitcast_fusion = f32[96,420,64]{1,2,0:T(8,128)} fusion(bf16[96,210,420]{1,2,0:T(8,128)(2,1)} %copy.13, bf16[96,210,64]{1,0,2:T(8,128)(2,1)} %reshape.53), kind=kOutput, calls=%fused_computation.12 | convolution fusion | flops 1083801600 | bytes 29836800 | tf_op jit(solution)/shard_map/ekb,ekr->ebr/dot_general | solution.py:35
  423.9 16.4 %copy.19 = f32[96,420,64]{1,0,2:T(8,128)} copy(f32[96,420,64]{1,2,0:T(8,128)} %convolution_bitcast_fusion) | data formatting | bytes 20643840 | tf_op jit(solution)/shard_map/ekb,ekr->ebr/dot_general | solution.py:35
  440.3 14.6 %reshape.107 = f32[384,105,64]{1,0,2:T(8,128)} reshape(f32[96,420,64]{1,0,2:T(8,128)} %copy.19) | data formatting | bytes 20643840 | tf_op jit(solution)/shard_map/reshape | solution.py:39
  454.9 16.4 %copy.20 = f32[384,105,64]{1,2,0:T(8,128)} copy(f32[384,105,64]{1,0,2:T(8,128)} %reshape.107) | data formatting | bytes 20643840 | tf_op jit(solution)/shard_map/reshape | solution.py:39
  475.4 59.4 %scatter_fusion.2 = f32[240,105,64]{1,2,0:T(8,128)} fusion(f32[240,105,64]{1,2,0:T(8,128)} %broadcast.46, s32[384]{0:T(512)S(1)} %reshape.89, f32[384,105,64]{1,2,0:T(8,128)} %copy.20), kind=kCustom, calls=%fused_computation.6 | custom fusion | flops 2580480 | bytes 30967296 | tf_op jit(solution)/shard_map/scatter-add | solution.py:38
  534.8 6.1 convert_element_type.40
  541.0 13.1 %reduce-scatter.5.cloned.1.call-done = bf16[240,105,32]{1,2,0:T(8,128)(2,1)} async-done(((bf16[240,105,64]{1,2,0:T(8,128)(2,1)}), bf16[240,105,32]{1,2,0:T(8,128)(2,1)}) %reduce-scatter.5.cloned.1.call-update) | async-done | bytes 1612816 | tf_op jit(solution)/shard_map/reduce_scatter | solution.py:43
  555.9 7.0 %all-to-all-start.3 = ((bf16[48,105,32]{1,2,0:T(8,128)(2,1)}), bf16[48,105,32]{1,2,0:T(8,128)(2,1)S(1)}, u32[]{:S(2)}, u32[]{:S(2)}) async-start(bf16[48,105,32]{1,2,0:T(8,128)(2,1)} %slice.37), calls=%async_computation.5 | async-start | bytes 786432 | tf_op jit(solution)/shard_map/all_to_all | solution.py:46
  566.4 9.5 %all-to-all-done.3 = bf16[48,105,32]{1,2,0:T(8,128)(2,1)S(1)} async-done(((bf16[48,105,32]{1,2,0:T(8,128)(2,1)}), bf16[48,105,32]{1,2,0:T(8,128)(2,1)S(1)}, u32[]{:S(2)}, u32[]{:S(2)}) %all-to-all-start.3) | async-done | bytes 322592 | tf_op jit(solution)/shard_map/all_to_all | solution.py:46
  576.9 6.9 %scatter_fusion.3 = f32[192,105,32]{1,2,0:T(8,128)} fusion(f32[192,105,32]{1,2,0:T(8,128)} %slice_convert_fusion, s32[48]{0:T(128)S(1)} %bitcast.30, f32[48,105,32]{1,2,0:T(8,128)} %convert_element_type.41), kind=kCustom, calls=%fused_computation.7 | custom fusion | flops 161280 | bytes 1935552 | tf_op jit(solution)/shard_map/scatter-add | solution.py:53
  586.7 38.8 %all-reduce = (f32[32]{0:T(128)S(1)}, f32[32]{0:T(128)S(1)}) all-reduce(f32[32]{0:T(128)S(1)} %get-tuple-element.4, f32[32]{0:T(128)S(1)} %get-tuple-element.3), channel_id=1, replica_groups=mesh['dom'=16,'col'=2] {'dom'}, use_global_device_ids=true, to_apply=%region_15.0 | all-reduce | flops 64 | bytes 512 | tf_op jit(solution)/shard_map/psum | solution.py:72
  (59 shorter events, 53.0 us)
Async XLA Ops:
  7.2 47.8 %copy-start.3 = (s32[1,48]{1,0:T(1,128)S(1)}, s32[1,48]{1,0:T(1,128)}, u32[]{:S(2)}) copy-start(s32[1,48]{1,0:T(1,128)} %param.7) | copy-start | bytes 580
  7.2 94.9 %all-gather.3.cloned.1.call-start = ((), (), s32[]{:S(2)}) async-start(), calls=%async_computation.6 | async-start | bytes 5898240 | tf_op jit(solution)/shard_map/all_gather | solution.py:29
  67.9 1.8 copy-start.2
  69.7 184.7 %reduce-scatter.3.cloned.1.call-start = ((), (), s32[]{:S(2)}) async-start(), calls=%async_computation.7 | async-start | bytes 5898240 | tf_op jit(solution)/shard_map/reduce_scatter | solution.py:43
  256.2 19.9 %all-to-all-start.1 = ((bf16[48,105,32]{1,2,0:T(8,128)(2,1)}), bf16[48,105,32]{1,2,0:T(8,128)(2,1)S(1)}, u32[]{:S(2)}, u32[]{:S(2)}) async-start(bf16[48,105,32]{1,2,0:T(8,128)(2,1)} %slice.35), calls=%async_computation.2 | async-start | bytes 786432 | tf_op jit(solution)/shard_map/all_to_all | solution.py:46
  263.0 130.9 %all-gather.5.cloned.1.call-start = ((), (), s32[]{:S(2)}) async-start(), calls=%async_computation.8 | async-start | bytes 5898240 | tf_op jit(solution)/shard_map/all_gather | solution.py:29
  276.1 6.2 copy-start
  367.0 258.5 %copy-start.1 = (bf16[192,105,32]{1,2,0:T(8,128)(2,1)}, bf16[192,105,32]{1,2,0:T(8,128)(2,1)S(1)}, u32[]{:S(2)}) copy-start(bf16[192,105,32]{1,2,0:T(8,128)(2,1)S(1)} %divide_convert_fusion) | copy-start | bytes 3870724
  382.3 171.8 %reduce-scatter.5.cloned.1.call-start = ((), (), s32[]{:S(2)}) async-start(), calls=%async_computation.9 | async-start | bytes 5898240 | tf_op jit(solution)/shard_map/reduce_scatter | solution.py:43
  555.9 20.1 %all-to-all-start.3 = ((bf16[48,105,32]{1,2,0:T(8,128)(2,1)}), bf16[48,105,32]{1,2,0:T(8,128)(2,1)S(1)}, u32[]{:S(2)}, u32[]{:S(2)}) async-start(bf16[48,105,32]{1,2,0:T(8,128)(2,1)} %slice.37), calls=%async_computation.5 | async-start | bytes 786432 | tf_op jit(solution)/shard_map/all_to_all | solution.py:46
  562.9 14.0 %copy-start.4 = (s32[1,48]{1,0:T(1,128)S(1)}, s32[1,48]{1,0:T(1,128)}, u32[]{:S(2)}) copy-start(s32[1,48]{1,0:T(1,128)} %param.7) | copy-start | bytes 580
  625.5 3.9 copy-start.5
  625.5 3.9 copy-start.6
  625.6 3.9 copy-start.7
Sparse Core Ops, SparseCore 0:
  69.8 11.3 all-gather.2
  243.6 10.7 reduce-scatter.2
  382.4 11.4 all-gather.4
  541.1 12.9 reduce-scatter.4
where the time goes:
time: 648 us; the launch traced here: 637 us
  blocking collectives  183 us (28%)
  other arithmetic  176 us (27%)
  local copies, waits for them, and re-layouts  169 us (26%)
  waiting for transfers between devices  54.7 us (8%)
  matrix products  26.5 us (4%)
  between operations  14.4 us (2%)
  starting transfers between devices  14 us (2%)
    scatter-add x2, other arithmetic, transposed(): jax.ops.segment_sum(partial_terms.reshape(element_count * slot_total, P_S...  119 us
    reshape x4, local copies, waits for them, and re-layouts, transposed(): partial_terms.reshape(element_count * slot_total, P_SIZE, known_traces.sh...  62.1 us
    psum x1, blocking collectives, body(): lax.psum(jnp.sum(residual * residual, axis=(0, 1)), 'dom') / entries  43.5 us
    psum x1, blocking collectives, body(): lax.psum(jnp.sum(first_float * first_image, axis=(0, 1)), 'dom') / entries  39 us
    psum x1, blocking collectives, body(): lax.psum((jnp.sum(first_float * second_image, axis=(0, 1)), jnp.sum(secon...  38.8 us
    psum x1, blocking collectives, body(): lax.psum(jnp.sum(projected * projected, axis=(0, 1)), 'dom') / entries  36.7 us
    dot_general x2, local copies, waits for them, and re-layouts, transposed(): jnp.einsum('ekb,ekr->ebr', element_blocks, picked, preferred_element_type...  32.8 us
    unnamed x18, local copies, waits for them, and re-layouts  32 us
  transfers between devices with their start and end apart: 6, of which 5 were waited for; matrix products, arithmetic and copies ran while one was open for 6% of the time, Pallas kernels for 0%

commit v1 on v0

v1 whole, which is shorter than its diff:
```python
import functools

import jax
import jax.numpy as jnp
from jax import lax
from jax.experimental import pallas as pl
from jax.experimental.pallas import tpu as pltpu
from jax.sharding import PartitionSpec as P

P_SIZE = 105
LANES = 128
MIB = 1 << 20
TOGETHER = 4

epsilon = 1e-06

f32 = jnp.float32
bf16 = jnp.bfloat16

VMEM = pl.BlockSpec(memory_space=pltpu.VMEM)
SMEM = pl.BlockSpec(memory_space=pltpu.SMEM)
ANY = pl.BlockSpec(memory_space=pl.ANY)


def lane_ids(rows):
    return lax.broadcasted_iota(jnp.int32, (rows, LANES), 1)


def stat_lanes(columns):
    rows = columns[0].shape[0]
    lanes = lane_ids(rows)
    block = jnp.zeros((rows, LANES), f32)
    lane = P_SIZE
    for value in columns:
        rest = value * 0.5
        for _ in range(3):
            part = rest.astype(bf16).astype(f32)
            block = jnp.where(lanes == lane, part, block)
            rest = rest - part
            lane += 1
    return block


def read_stat(block, which):
    lanes = lane_ids(block.shape[0])
    first = P_SIZE + 3 * which
    inside = (lanes >= first) & (lanes < first + 3)
    return 2.0 * jnp.sum(jnp.where(inside, block, 0.0), axis=1, keepdims=True)


def gathered_block(ghost_ref, ranks):
    slots = ghost_ref.shape[0] // ranks
    total = ghost_ref[0].astype(f32)
    for rank in range(1, ranks):
        total = total + ghost_ref[rank * slots].astype(f32)
    return total


def first_payload_kernel(rhs_ref, send_ref, payload_ref):
    faces, rows, _ = rhs_ref.shape

    def add(step, total):
        chunk = rhs_ref[pl.ds(step * 8, 8)].astype(f32)
        return total + jnp.sum(chunk * chunk, axis=0)

    total = lax.fori_loop(0, faces // 8, add, jnp.zeros((rows, P_SIZE), f32))
    stats = stat_lanes([jnp.sum(total, axis=1, keepdims=True)]).astype(bf16)

    @pl.loop(0, payload_ref.shape[0])
    def _(slot):
        payload_ref[slot] = stats
        payload_ref[slot, :, :P_SIZE] = rhs_ref[send_ref[0, slot]]


def relayout_kernel(raw_ref, perm_ref, tail_ref, out_ref, buffer, sems):
    group = buffer.shape[2]
    steps = raw_ref.shape[1] // group
    width = out_ref.shape[2]
    contracted = raw_ref.shape[0]
    slots = contracted // P_SIZE
    full = P_SIZE // group
    rest = P_SIZE - full * group

    def copy(step):
        return pltpu.make_async_copy(
            raw_ref.at[:, pl.ds(pl.multiple_of(step * group, group), group), :], buffer.at[step % 2], sems.at[step % 2]
        )

    copy(0).start()

    @pl.loop(0, steps)
    def _(step):
        @pl.when(step + 1 < steps)
        def _():
            copy(step + 1).start()

        copy(step).wait()
        held = buffer.at[step % 2]
        for slot in range(slots):
            for part in range(full + 1):
                first = slot * P_SIZE + part * group
                depth = group if part < full else rest
                chunk = held[first : first + depth].reshape(depth * group, raw_ref.shape[2])
                perm = perm_ref[...] if part < full else tail_ref[...]
                moved = jnp.dot(perm, chunk, preferred_element_type=f32).astype(bf16)
                for element in range(group):
                    out_ref[
                        step * group + element, pl.ds(slot * LANES + part * group, group), : raw_ref.shape[2]
                    ] = moved[element * group : (element + 1) * group]
        zeros = jnp.zeros((LANES - (full + 1) * group, width), bf16)
        for element in range(group):
            for slot in range(slots):
                out_ref[step * group + element, pl.ds(slot * LANES + (full + 1) * group, zeros.shape[0]), :] = zeros


def apply_operator(basis_ref, blocks_ref, faces_ref, first_slot, sums_ref, buffer=None, sems=None):
    elements = blocks_ref.shape[0]
    rows = basis_ref.shape[1]
    together = TOGETHER
    steps = elements // together
    lanes = lane_ids(rows)

    def copy(step):
        return pltpu.make_async_copy(
            blocks_ref.at[pl.ds(step * together, together)], buffer.at[step % 2], sems.at[step % 2]
        )

    if buffer is not None:
        copy(0).start()

    @pl.loop(0, sums_ref.shape[0])
    def _(slot):
        sums_ref[slot] = jnp.zeros((rows, LANES), f32)

    @pl.loop(0, steps)
    def _(step):
        if buffer is not None:

            @pl.when(step + 1 < steps)
            def _():
                copy(step + 1).start()

            copy(step).wait()
        pieces = []
        for inner in range(together):
            element = step * together + inner
            left = basis_ref[faces_ref[first_slot, element]]
            right = basis_ref[faces_ref[first_slot + 1, element]]
            block = blocks_ref[element] if buffer is None else buffer[step % 2, inner]
            terms = jnp.dot(jnp.concatenate([left, right], axis=1), block, preferred_element_type=f32)
            tiles = [terms[:, LANES * n : LANES * (n + 1)] for n in range(4)]
            for slot in range(4):
                if slot == 0:
                    piece = tiles[0]
                else:
                    shift = slot * (LANES - P_SIZE)
                    piece = jnp.where(
                        lanes < shift, pltpu.roll(tiles[slot - 1], shift, 1), pltpu.roll(tiles[slot], shift, 1)
                    )
                pieces.append((faces_ref[slot, element], piece))
        for slot, piece in pieces:
            sums_ref[slot] += piece


def write_sums(sums_ref, bases, own_ref, other_ref, ghost_own_ref, ghost_other_ref):
    owned, half, _ = own_ref.shape
    rows = sums_ref.shape[1]
    ghosts = ghost_own_ref.shape[0]
    inside = lane_ids(rows) < P_SIZE

    def rounded(slot):
        return jnp.where(inside, sums_ref[slot], 0.0).astype(bf16)

    def add_dots(slot, value, dots):
        wide = value.astype(f32)
        return tuple(dot + basis[slot].astype(f32) * wide for dot, basis in zip(dots, bases))

    def owned_step(slot, dots):
        value = rounded(slot)
        own_ref[slot] = value[:half]
        other_ref[slot] = value[half:]
        return add_dots(slot, value, dots)

    def ghost_step(slot, dots):
        return add_dots(owned + slot, rounded(owned + slot), dots)

    dots = tuple(jnp.zeros((rows, LANES), f32) for _ in bases)
    dots = lax.fori_loop(0, owned, owned_step, dots, unroll=2)
    dots = lax.fori_loop(0, ghosts, ghost_step, dots, unroll=2)
    stats = stat_lanes([jnp.sum(dot, axis=1, keepdims=True) for dot in dots])

    @pl.loop(0, ghosts)
    def _(slot):
        value = jnp.where(inside, sums_ref[owned + slot], stats).astype(bf16)
        ghost_own_ref[slot] = value[:half]
        ghost_other_ref[slot] = value[half:]


def first_apply_kernel(
    ranks, entries, rhs_ref, rhs_other_ref, ghost_ref, ghost_other_ref, blocks_ref, faces_ref,
    basis_ref, own_ref, other_ref, ghost_own_out, ghost_other_out, norm_ref, sums_ref, *stream,
):
    owned, half, _ = rhs_ref.shape
    ghosts = ghost_ref.shape[0]
    inside = lane_ids(half) < P_SIZE

    def inverse_norm(ref):
        return jnp.sqrt(read_stat(gathered_block(ref, ranks), 0) / entries + epsilon)

    norm = inverse_norm(ghost_ref)
    norm_ref[...] = jnp.broadcast_to(norm, (half, LANES))
    scale = 1.0 / norm
    scale_other = 1.0 / inverse_norm(ghost_other_ref)

    @pl.loop(0, owned)
    def _(face):
        basis_ref[face] = jnp.zeros(basis_ref.shape[1:], bf16)
        basis_ref[face, :half, :P_SIZE] = (rhs_ref[face].astype(f32) * scale).astype(bf16)
        basis_ref[face, half:, :P_SIZE] = (rhs_other_ref[face].astype(f32) * scale_other).astype(bf16)

    @pl.loop(0, ghosts)
    def _(slot):
        basis_ref[owned + slot, :half] = jnp.where(inside, ghost_ref[slot].astype(f32) * scale, 0.0).astype(bf16)
        basis_ref[owned + slot, half:] = jnp.where(
            inside, ghost_other_ref[slot].astype(f32) * scale_other, 0.0
        ).astype(bf16)

    apply_operator(basis_ref, blocks_ref, faces_ref, 2 * lax.axis_index("col"), sums_ref, *stream)
    write_sums(sums_ref, [basis_ref], own_ref, other_ref, ghost_own_out, ghost_other_out)


def return_payload_kernel(stats, own_ref, other_ref, payload_ref):
    half = own_ref.shape[1]
    inside = lane_ids(half) < P_SIZE
    sums = own_ref[0].astype(f32) + other_ref[0].astype(f32)
    lanes = stat_lanes(
        [read_stat(own_ref[0].astype(f32), n) + read_stat(other_ref[0].astype(f32), n) for n in range(stats)]
    )

    @pl.loop(0, payload_ref.shape[0])
    def _(slot):
        total = own_ref[slot].astype(f32) + other_ref[slot].astype(f32)
        payload_ref[slot] = jnp.where(inside, total, lanes).astype(bf16)


def project_kernel(
    ranks, entries, own_ref, other_ref, returned_ref, basis_ref, send_ref,
    projected_ref, rounded_ref, payload_ref, diagonal_ref,
):
    owned, half, _ = own_ref.shape
    inside = lane_ids(half) < P_SIZE
    diagonal = read_stat(gathered_block(returned_ref, ranks), 0) / entries
    diagonal_ref[...] = jnp.broadcast_to(diagonal, (half, LANES))

    @pl.loop(0, owned)
    def _(face):
        projected_ref[face] = (
            own_ref[face].astype(f32)
            + other_ref[face].astype(f32)
            - diagonal * basis_ref[face, :half].astype(f32)
        )

    @pl.loop(0, payload_ref.shape[0])
    def _(slot):
        projected_ref[send_ref[0, slot]] += jnp.where(inside, returned_ref[slot].astype(f32), 0.0)

    def round_step(face, total):
        value = projected_ref[face]
        rounded_ref[face] = value.astype(bf16)
        return total + value * value

    total = lax.fori_loop(0, owned, round_step, jnp.zeros((half, LANES), f32), unroll=2)
    stats = stat_lanes([jnp.sum(total, axis=1, keepdims=True)]).astype(bf16)

    @pl.loop(0, payload_ref.shape[0])
    def _(slot):
        payload_ref[slot] = jnp.where(inside, rounded_ref[send_ref[0, slot]], stats)


def second_apply_kernel(
    ranks, entries, projected_ref, rounded_other_ref, ghost_ref, ghost_other_ref, blocks_ref, faces_ref, first_ref,
    second_ref, own_ref, other_ref, ghost_own_out, ghost_other_out, norm_ref, basis_ref, sums_ref, *stream,
):
    owned, half, _ = projected_ref.shape
    ghosts = ghost_ref.shape[0]
    inside = lane_ids(half) < P_SIZE

    def next_norm(ref):
        return jnp.sqrt(read_stat(gathered_block(ref, ranks), 0) / entries + epsilon)

    norm = next_norm(ghost_ref)
    norm_ref[...] = jnp.broadcast_to(norm, (half, LANES))
    scale = 1.0 / norm
    scale_other = 1.0 / next_norm(ghost_other_ref)

    @pl.loop(0, owned)
    def _(face):
        value = (projected_ref[face] * scale).astype(bf16)
        basis_ref[face, :half] = value
        second_ref[face] = value[:, :P_SIZE]
        basis_ref[face, half:] = (rounded_other_ref[face].astype(f32) * scale_other).astype(bf16)

    @pl.loop(0, ghosts)
    def _(slot):
        basis_ref[owned + slot, :half] = jnp.where(inside, ghost_ref[slot].astype(f32) * scale, 0.0).astype(bf16)
        basis_ref[owned + slot, half:] = jnp.where(
            inside, ghost_other_ref[slot].astype(f32) * scale_other, 0.0
        ).astype(bf16)

    apply_operator(basis_ref, blocks_ref, faces_ref, 2 * lax.axis_index("col"), sums_ref, *stream)
    write_sums(sums_ref, [first_ref, basis_ref], own_ref, other_ref, ghost_own_out, ghost_other_out)


def final_kernel(
    ranks, entries, own_ref, other_ref, returned_ref, first_ref, second_ref, send_ref, start_ref, diagonal_ref, next_ref,
    vector_ref, hessenberg_ref, image_ref,
):
    owned, half, _ = own_ref.shape
    block = gathered_block(returned_ref, ranks)
    proj_first = read_stat(block, 0) / entries
    proj_second = read_stat(block, 1) / entries

    @pl.loop(0, owned)
    def _(face):
        image_ref[face] = own_ref[face].astype(f32) + other_ref[face].astype(f32)

    @pl.loop(0, returned_ref.shape[0])
    def _(slot):
        image_ref[send_ref[0, slot]] += returned_ref[slot].astype(f32)

    @pl.loop(0, owned)
    def _(face):
        value = (
            image_ref[face][:, :P_SIZE]
            - proj_first * first_ref[face, :half, :P_SIZE].astype(f32)
            - proj_second * second_ref[face].astype(f32)
        )
        vector_ref[face] = value.astype(bf16)

    lanes = lane_ids(half)
    table = jnp.zeros((half, LANES), f32)
    for row, value in enumerate(
        [start_ref[...], diagonal_ref[...], next_ref[...], proj_first, proj_second]
    ):
        table = jnp.where(lanes == row, value, table)
    hessenberg_ref[...] = jnp.transpose(table)[: hessenberg_ref.shape[0]]


def call(kernel, out_shape, in_specs, scratch=(), limit=16, flops=0, bytes_accessed=0, **kwargs):
    return pl.pallas_call(
        kernel,
        out_shape=out_shape,
        in_specs=in_specs,
        scratch_shapes=scratch,
        compiler_params=pltpu.CompilerParams(vmem_limit_bytes=limit * MIB),
        cost_estimate=pl.CostEstimate(flops=flops, bytes_accessed=bytes_accessed, transcendentals=0),
        **kwargs,
    )


def body(adjoint_rhs, element_blocks, element_faces, send_faces):
    ranks = lax.axis_size("dom")
    rhs = jnp.transpose(adjoint_rhs, (0, 2, 1))
    owned, half, _ = rhs.shape
    entries = float(ranks * owned * P_SIZE)
    ghosts = send_faces.shape[1]
    elements, contracted, block_width = element_blocks.shape
    slots = owned + ghosts
    faces = element_faces.T
    raw = jnp.transpose(element_blocks, (1, 0, 2))
    group = 16
    rest = P_SIZE % group
    width = -(-block_width // LANES) * LANES
    work = -(-slots * 2 * half * LANES * 4 // MIB)
    spare = 5 - (-ghosts * half * LANES * 8 // MIB)

    held = elements * 2 * LANES * width * 2 + slots * 2 * half * LANES * 10
    resident = held <= 44 * MIB
    stream = []
    if not resident:
        stream = [pltpu.VMEM((2, TOGETHER, 2 * LANES, width), bf16), pltpu.SemaphoreType.DMA((2,))]
        spare += 2 * TOGETHER

    def out(shape, dtype=bf16):
        return pltpu.VMEM(shape, dtype) if resident else jax.ShapeDtypeStruct(shape, dtype)

    def swap(value):
        return lax.ppermute(value, "col", [(0, 1), (1, 0)])

    def exchange(value):
        return lax.all_to_all(value, "dom", split_axis=0, concat_axis=0, tiled=True)

    rhs_other = swap(rhs)

    payload = call(first_payload_kernel, out((ghosts, half, LANES)), [VMEM, SMEM])(rhs, send_faces)
    ghost = exchange(payload)

    row = jnp.arange(group * group)
    column = jnp.arange(group * group)
    perm = ((row[:, None] // group == column[None, :] % group) & (row[:, None] % group == column[None, :] // group))
    perm = perm.astype(bf16)
    tail = perm[:, : rest * group]
    blocks = call(
        relayout_kernel,
        out((elements, 2 * LANES, width)),
        [ANY, VMEM, VMEM],
        [pltpu.VMEM((2, contracted, group, block_width), bf16), pltpu.SemaphoreType.DMA((2,))],
        limit=14 if resident else 40,
        flops=2 * 256 * 256 * 512 * 84,
        bytes_accessed=2 * raw.size,
    )(raw, perm, tail)
    if resident:
        blocks = pltpu.with_memory_space_constraint(blocks, pltpu.VMEM)
    held_blocks = VMEM if resident else ANY

    ghost_other = swap(ghost)

    field = out((owned, half, LANES))
    ghost_field = out((ghosts, half, LANES))
    column_values = out((half, LANES), f32)
    sums = pltpu.VMEM((slots, 2 * half, LANES), f32)
    first_basis, own, other, ghost_own, ghost_cross, start_norm = call(
        functools.partial(first_apply_kernel, ranks, entries),
        (out((slots, 2 * half, LANES)), field, field, ghost_field, ghost_field, column_values),
        [VMEM] * 4 + [held_blocks, SMEM],
        [sums] + stream,
        limit=work + spare,
    )(rhs, rhs_other, ghost, ghost_other, blocks, faces)

    ghost_cross = swap(ghost_cross)
    other = swap(other)
    payload = call(functools.partial(return_payload_kernel, 1), ghost_field, [VMEM, VMEM])(ghost_own, ghost_cross)
    returned = exchange(payload)

    projected, rounded, payload, diagonal = call(
        functools.partial(project_kernel, ranks, entries),
        (out((owned, half, LANES), f32), field, ghost_field, column_values),
        [VMEM] * 4 + [SMEM],
    )(own, other, returned, first_basis, send_faces)

    rounded_other = swap(rounded)
    ghost = exchange(payload)
    ghost_other = swap(ghost)

    second, own, other, ghost_own, ghost_cross, next_norm = call(
        functools.partial(second_apply_kernel, ranks, entries),
        (out((owned, half, P_SIZE)), field, field, ghost_field, ghost_field, column_values),
        [VMEM] * 4 + [held_blocks, SMEM, VMEM],
        [pltpu.VMEM((slots, 2 * half, LANES), bf16), sums] + stream,
        limit=work + work // 2 + spare,
    )(projected, rounded_other, ghost, ghost_other, blocks, faces, first_basis)

    ghost_cross = swap(ghost_cross)
    other = swap(other)
    payload = call(functools.partial(return_payload_kernel, 2), ghost_field, [VMEM, VMEM])(ghost_own, ghost_cross)
    returned = exchange(payload)

    vector, hessenberg = call(
        functools.partial(final_kernel, ranks, entries),
        (jax.ShapeDtypeStruct((owned, half, P_SIZE), bf16), jax.ShapeDtypeStruct((5, half), f32)),
        [VMEM] * 5 + [SMEM] + [VMEM] * 3,
        [pltpu.VMEM((owned, half, LANES), f32)],
    )(own, other, returned, first_basis, second, send_faces, start_norm, diagonal, next_norm)

    return (jnp.transpose(second, (0, 2, 1)), jnp.transpose(vector, (0, 2, 1)), hessenberg)


def solution(mesh):
    in_specs = (P("dom", None, "col"), P("dom", "col", None), P("dom", None), P("dom", None))
    out_specs = (P("dom", None, "col"), P("dom", None, "col"), P(None, "col"))
    return jax.shard_map(body, mesh=mesh, in_specs=in_specs, out_specs=out_specs, check_vma=False)
```

time: 648 us -> 161 us (0.25); the launches traced: 637 us -> 160 us
  other arithmetic: 176 us -> 0.14 us
  local copies, waits for them, and re-layouts: 169 us -> 16.9 us
  blocking collectives: 183 us -> 33.2 us
  Pallas kernels: 0 us -> 61.7 us
  matrix products: 26.5 us -> 0 us
  waiting for transfers between devices: 54.7 us -> 33.5 us
  between operations: 14.4 us -> 0.82 us
    psum x4 -> x0, blocking collectives: 158 us -> none  [the longest x1 43.5 us: body(): lax.psum(jnp.sum(residual * residual, axis=(0, 1)), 'dom') / entries]
    scatter-add x4 -> x0, other arithmetic: 132 us -> none  [the longest x2 119 us: transposed(): jax.ops.segment_sum(partial_terms.reshape(element_count * slot_total, P_S...]
    reshape x6 -> x0, local copies, waits for them, and re-layouts: 72.4 us -> none  [the longest x4 62.1 us: transposed(): partial_terms.reshape(element_count * slot_total, P_SIZE, known_traces.sh...]
    pallas_call x0 -> x8, Pallas kernels: none -> 61.7 us  [the longest x1 21 us: body(): call(functools.partial(second_apply_kernel, ranks, entries), (out((owned,...]
    dot_general x2 -> x0, local copies, waits for them, and re-layouts: 32.8 us -> none  [transposed(): jnp.einsum('ekb,ekr->ebr', element_blocks, picked, preferred_element_type...]
    dot_general x2 -> x0, matrix products: 26.5 us -> none  [transposed(): jnp.einsum('ekb,ekr->ebr', element_blocks, picked, preferred_element_type...]
    reduce_scatter x2 -> x0, waiting for transfers between devices: 24.1 us -> none  [transposed(): lax.psum_scatter(summed.astype(jnp.bfloat16), 'col', scatter_dimension=2,...]
    convert_element_type x7 -> x1, other arithmetic: 21.6 us -> 0.13 us  [body(): perm = perm.astype(bf16)]
  transfers between devices with their start and end apart: 6 -> 10, of which waited for: 5 -> 5; matrix products, arithmetic and copies ran while one was open for 6% -> 1% of each run, Pallas kernels for 0% -> 9%
where the time goes in v1:
time: 161 us; the launch traced here: 160 us
  Pallas kernels  61.7 us (38%)
  waiting for transfers between devices  33.5 us (21%)
  blocking collectives  33.2 us (21%)
  local copies, waits for them, and re-layouts  16.9 us (10%)
  starting transfers between devices  13.3 us (8%)
    all_to_all x2, blocking collectives, exchange(): return lax.all_to_all(value, 'dom', split_axis=0, concat_axis=0, tiled=True)  33.2 us
    all_to_all x2, waiting for transfers between devices, exchange(): return lax.all_to_all(value, 'dom', split_axis=0, concat_axis=0, tiled=True)  25.1 us
    pallas_call x1, Pallas kernels, body(): call(functools.partial(second_apply_kernel, ranks, entries), (out((owned,...  21 us
    pallas_call x1, Pallas kernels, body(): call(functools.partial(first_apply_kernel, ranks, entries), (out((slots,...  17.4 us
    unnamed x31, local copies, waits for them, and re-layouts  16.9 us
    all_to_all x2, starting transfers between devices, exchange(): return lax.all_to_all(value, 'dom', split_axis=0, concat_axis=0, tiled=True)  11.6 us
    pallas_call x1, Pallas kernels, body(): call(relayout_kernel, out((elements, 2 * LANES, width)), [ANY, VMEM, VMEM...  10.9 us
    ppermute x8, waiting for transfers between devices, swap(): return lax.ppermute(value, 'col', [(0, 1), (1, 0)])  8.48 us
  transfers between devices with their start and end apart: 10, of which 5 were waited for; matrix products, arithmetic and copies ran while one was open for 1% of the time, Pallas kernels for 9%

profile of v1, /device:TPU:0, one launch (start us, length us, event | category | flops | bytes accessed | tf_op | source)
XLA Modules:
  0.0 159.8 jit_solution(6476759530013782036)
XLA Ops:
  0.6 0.5 collective-permute-start
  1.1 1.4 copy-done.4
  2.6 0.7 copy-done.12
  3.2 2.2 %shard_map.67 = bf16[48,32,128]{2,1,0:T(8,128)(2,1)} custom-call(bf16[192,32,105]{2,1,0:T(8,128)(2,1)S(1)} %bitcast.8, s32[1,48]{1,0:T(1,128)S(1)} %copy-done.12), custom_call_target="tpu_custom_call" | custom-call | tf_op jit(solution)/shard_map/pallas_call | solution.py:395
  5.4 7.9 %all-to-all-start = ((bf16[48,32,128]{2,1,0:T(8,128)(2,1)}), bf16[48,32,128]{2,1,0:T(8,128)(2,1)S(1)}, u32[]{:S(2)}, u32[]{:S(2)}) async-start(bf16[48,32,128]{2,1,0:T(8,128)(2,1)} %shard_map.67), calls=%async_computation | async-start | bytes 786432 | tf_op jit(solution)/shard_map/all_to_all | solution.py:391
  13.3 0.1 and_convert_fusion.perm_ref
  13.5 13.0 %all-to-all-done.ghost_ref = bf16[48,32,128]{2,1,0:T(8,128)(2,1)S(1)} async-done(((bf16[48,32,128]{2,1,0:T(8,128)(2,1)}), bf16[48,32,128]{2,1,0:T(8,128)(2,1)S(1)}, u32[]{:S(2)}, u32[]{:S(2)}) %all-to-all-start) | async-done | bytes 393248 | tf_op jit(solution)/shard_map/all_to_all | solution.py:391
  26.5 10.9 %shard_map.68.blocks_ref = bf16[96,256,512]{2,1,0:T(8,128)(2,1)S(1)} custom-call(bf16[210,96,420]{2,1,0:T(8,128)(2,1)} %bitcast.13, bf16[256,256]{1,0:T(8,128)(2,1)S(1)} %and_convert_fusion.perm_ref, bf16[256,144]{1,0:T(8,128)(2,1)S(1)} %bitcast.10), custom_call_target="tpu_custom_call" | custom-call | flops 5637144576 | bytes 16934400 | tf_op jit(solution)/shard_map/pallas_call | solution.py:403
  37.5 17.4 %shard_map.69 = (bf16[240,64,128]{2,1,0:T(8,128)(2,1)S(1)}, bf16[192,32,128]{2,1,0:T(8,128)(2,1)S(1)}, bf16[192,32,128]{2,1,0:T(8,128)(2,1)S(1)}, bf16[48,32,128...) custom-call(bf16[192,32,105]{2,1,0:T(8,128)(2,1)S(1)} %bitcast.9, ...), custom_call_target="tpu_custom_call" | custom-call | tf_op jit(solution)/shard_map/pallas_call | solution.py:422
  54.9 0.6 collective-permute-start.2
  55.6 3.5 %collective-permute-done.3.other_ref = bf16[48,32,128]{2,1,0:T(8,128)(2,1)S(1)} collective-permute-done((bf16[48,32,128]{2,1,0:T(8,128)(2,1)S(1)}, bf16[48,32,128]{2,1,0:T(8,128)(2,1)S(1)}, u32[]{:S(2)}, u32[]{:S(2)}) %collective-permute-start.3) | collective-permute-done | bytes 393248 | tf_op jit(solution)/shard_map/ppermute | solution.py:388
  59.1 0.4 shard_map.70
  59.5 16.6 %all_to_all.20.returned_ref = bf16[48,32,128]{2,1,0:T(8,128)(2,1)S(1)} all-to-all(bf16[48,32,128]{2,1,0:T(8,128)(2,1)S(1)} %shard_map.70), channel_id=1, replica_groups=mesh['dom'=16,'col'=2] {'dom'}, dimensions={0} | all-to-all | bytes 786432 | tf_op jit(solution)/shard_map/all_to_all | solution.py:391
  76.1 3.6 %shard_map.71 = (f32[192,32,128]{2,1,0:T(8,128)S(1)}, bf16[192,32,128]{2,1,0:T(8,128)(2,1)S(1)}, bf16[48,32,128]{2,1,0:T(8,128)(2,1)S(1)}, f32[32,128]{1,0:T(8,128)S(1)}) custom-call(bf16[192,32,128]{2,1,0:T(8,128)(2,1)S(1)} %get-tuple-element.21.own_ref, bf16[192,32,128]{2,1,0:T(8,128)(2,1)S(1)} %collective-permute-done.2.other_ref, ...), custom_call_target="tpu_custom_call" | custom-call | tf_op jit(solution)/shard_map/pallas_call | solution.py:435
  79.8 16.6 %all_to_all.21.ghost_ref = bf16[48,32,128]{2,1,0:T(8,128)(2,1)S(1)} all-to-all(bf16[48,32,128]{2,1,0:T(8,128)(2,1)S(1)} %get-tuple-element.28), channel_id=1, replica_groups=mesh['dom'=16,'col'=2] {'dom'}, dimensions={0} | all-to-all | bytes 786432 | tf_op jit(solution)/shard_map/all_to_all | solution.py:391
  96.4 1.7 %collective-permute-done.5.ghost_other_ref = bf16[48,32,128]{2,1,0:T(8,128)(2,1)S(1)} collective-permute-done((bf16[48,32,128]{2,1,0:T(8,128)(2,1)S(1)}, bf16[48,32,128]{2,1,0:T(8,128)(2,1)S(1)}, u32[]{:S(2)}, u32[]{:S(2)}) %collective-permute-start.5) | collective-permute-done | bytes 393248 | tf_op jit(solution)/shard_map/ppermute | solution.py:388
  98.2 8.2 %copy-done.1 = bf16[96,256,512]{2,1,0:T(8,128)(2,1)S(1)} copy-done((bf16[96,256,512]{2,1,0:T(8,128)(2,1)S(1)}, bf16[96,256,512]{2,1,0:T(8,128)(2,1)}, u32[]{:S(2)}) %copy-start.1) | copy-done | bytes 25165848
  106.3 21.0 %shard_map.72 = (bf16[192,32,105]{2,1,0:T(8,128)(2,1)S(1)}, bf16[192,32,128]{2,1,0:T(8,128)(2,1)S(1)}, bf16[192,32,128]{2,1,0:T(8,128)(2,1)}, bf16[48,32,128]{2,...) custom-call(f32[192,32,128]{2,1,0:T(8,128)S(1)} %get-tuple-element.26.projected_ref, ...), custom_call_target="tpu_custom_call" | custom-call | tf_op jit(solution)/shard_map/pallas_call | solution.py:445
  127.3 0.6 copy-done.9
  127.9 0.1 collective-permute-start.6
  128.1 0.4 collective-permute-start.7
  128.4 3.2 %collective-permute-done.7.other_ref = bf16[48,32,128]{2,1,0:T(8,128)(2,1)S(1)} collective-permute-done((bf16[48,32,128]{2,1,0:T(8,128)(2,1)S(1)}, bf16[48,32,128]{2,1,0:T(8,128)(2,1)S(1)}, u32[]{:S(2)}, u32[]{:S(2)}) %collective-permute-start.7) | collective-permute-done | bytes 393248 | tf_op jit(solution)/shard_map/ppermute | solution.py:388
  131.7 0.4 shard_map.73
  132.1 0.8 copy-done.6
  132.8 3.7 %all-to-all-start.3 = ((bf16[48,32,128]{2,1,0:T(8,128)(2,1)}), bf16[48,32,128]{2,1,0:T(8,128)(2,1)S(1)}, u32[]{:S(2)}, u32[]{:S(2)}) async-start(bf16[48,32,128]{2,1,0:T(8,128)(2,1)} %copy-done.6), calls=%async_computation.3 | async-start | bytes 786432 | tf_op jit(solution)/shard_map/all_to_all | solution.py:391
  136.6 1.1 copy.7
  137.7 12.0 %all-to-all-done.3.returned_ref = bf16[48,32,128]{2,1,0:T(8,128)(2,1)S(1)} async-done(((bf16[48,32,128]{2,1,0:T(8,128)(2,1)}), bf16[48,32,128]{2,1,0:T(8,128)(2,1)S(1)}, u32[]{:S(2)}, u32[]{:S(2)}) %all-to-all-start.3) | async-done | bytes 393248 | tf_op jit(solution)/shard_map/all_to_all | solution.py:391
  149.7 2.1 %copy-done.3 = bf16[240,64,128]{2,1,0:T(8,128)(2,1)S(1)} copy-done((bf16[240,64,128]{2,1,0:T(8,128)(2,1)S(1)}, bf16[240,64,128]{2,1,0:T(8,128)(2,1)}, u32[]{:S(2)}) %copy-start.3) | copy-done | bytes 3932184
  151.9 0.7 copy-done.8
  152.6 0.7 copy-done.10
  153.3 0.7 copy-done.14
  154.0 5.8 %shard_map.74 = (bf16[192,32,105]{2,1,0:T(8,128)(2,1)}, f32[5,32]{1,0:T(8,128)}) custom-call(bf16[192,32,128]{2,1,0:T(8,128)(2,1)S(1)} %get-tuple-element.30.own_ref, bf16[192,32,128]{2,1,0:T(8,128)(2,1)} %collective-permute-done.6.other_ref, bf16[48,32,128]{2,1,0:T(8,128)(2,1)S(1)} %all-to-all-done.3.returned_ref, bf16[240,64,128]{2,1,0:T(8,128)(2,1)S(1)} %copy-done.3, ...), custom_call_target="tpu_custom_call" | custom-call | tf_op jit(solution)/shard_map/pallas_call | solution.py:458
  (31 shorter events, 0.2 us)
Async XLA Ops:
  0.6 36.8 %collective-permute-start = (bf16[192,32,105]{2,1,0:T(8,128)(2,1)}, bf16[192,32,105]{2,1,0:T(8,128)(2,1)S(1)}, u32[]{:S(2)}, u32[]{:S(2)}) collective-permute-start(bf16[192,32,105]{2,1,0:T(8,128)(2,1)} %bitcast.7), channel_id=1, source_target_pairs={{0,1},{1,0},{2,3},{3,2},{4,5},{5,4},{6,7},{7,6},{8,9},{9,8},{10,11... | collective-permute-start | bytes 3870728 | tf_op jit(solution)/shard_map/ppermute | solution.py:388
  1.1 1.4 copy-start.4
  2.6 0.7 copy-start.12
  5.4 21.1 %all-to-all-start = ((bf16[48,32,128]{2,1,0:T(8,128)(2,1)}), bf16[48,32,128]{2,1,0:T(8,128)(2,1)S(1)}, u32[]{:S(2)}, u32[]{:S(2)}) async-start(bf16[48,32,128]{2,1,0:T(8,128)(2,1)} %shard_map.67), calls=%async_computation | async-start | bytes 786432 | tf_op jit(solution)/shard_map/all_to_all | solution.py:391
  26.5 11.0 %collective-permute-start.1 = (bf16[48,32,128]{2,1,0:T(8,128)(2,1)S(1)}, bf16[48,32,128]{2,1,0:T(8,128)(2,1)S(1)}, u32[]{:S(2)}, u32[]{:S(2)}) collective-permute-start(bf16[48,32,128]{2,1,0:T(8,128)(2,1)S(1)} %all-to-all-done.ghost_ref), channel_id=1, source_target_pairs={{0,1},{1,0},{2,3},{3,2},{4,5},{5,4},{6,7},{7,6},{8,9},{9,8},{10,11... | collective-permute-start | bytes 1179656 | tf_op jit(solution)/shard_map/ppermute | solution.py:388
  26.5 11.0 %copy-start.5 = (bf16[192,105,32]{1,2,0:T(8,128)(2,1)S(1)}, bf16[192,105,32]{1,2,0:T(8,128)(2,1)}, u32[]{:S(2)}) copy-start(bf16[192,105,32]{1,2,0:T(8,128)(2,1)} %param.4) | copy-start | bytes 3870724
  26.5 11.0 %copy-start.11 = (s32[96,4]{0,1:T(4,128)S(1)}, s32[96,4]{0,1:T(4,128)}, u32[]{:S(2)}) copy-start(s32[96,4]{0,1:T(4,128)} %param.6) | copy-start | bytes 4612
  37.4 17.5 %copy-start = (bf16[96,256,512]{2,1,0:T(8,128)(2,1)}, bf16[96,256,512]{2,1,0:T(8,128)(2,1)S(1)}, u32[]{:S(2)}) copy-start(bf16[96,256,512]{2,1,0:T(8,128)(2,1)S(1)} %shard_map.68.blocks_ref) | copy-start | bytes 75497472
  54.9 24.8 %copy-start.2 = (bf16[240,64,128]{2,1,0:T(8,128)(2,1)}, bf16[240,64,128]{2,1,0:T(8,128)(2,1)S(1)}, u32[]{:S(2)}) copy-start(bf16[240,64,128]{2,1,0:T(8,128)(2,1)S(1)} %get-tuple-element.25.basis_ref.first_ref) | copy-start | bytes 11796484
  54.9 21.2 %copy-start.13 = (s32[1,48]{1,0:T(1,128)S(1)}, s32[1,48]{1,0:T(1,128)}, u32[]{:S(2)}) copy-start(s32[1,48]{1,0:T(1,128)} %send_ref.5) | copy-start | bytes 580
  54.9 21.2 %collective-permute-start.2 = (bf16[192,32,128]{2,1,0:T(8,128)(2,1)S(1)}, bf16[192,32,128]{2,1,0:T(8,128)(2,1)S(1)}, u32[]{:S(2)}, u32[]{:S(2)}) collective-permute-start(bf16[192,32,128]{2,1,0:T(8,128)(2,1)S(1)} %get-tuple-element.22), channel_id=1, source_target_pairs={{0,1},{1,0},{2,3},{3,2},{4,5},{5,4},{6,7},{7,6},{8,9},{9,8},{10,11... | collective-permute-start | bytes 4718600 | tf_op jit(solution)/shard_map/ppermute | solution.py:388
  55.5 3.6 %collective-permute-start.3 = (bf16[48,32,128]{2,1,0:T(8,128)(2,1)S(1)}, bf16[48,32,128]{2,1,0:T(8,128)(2,1)S(1)}, u32[]{:S(2)}, u32[]{:S(2)}) collective-permute-start(bf16[48,32,128]{2,1,0:T(8,128)(2,1)S(1)} %get-tuple-element.24), channel_id=1, source_target_pairs={{0,1},{1,0},{2,3},{3,2},{4,5},{5,4},{6,7},{7,6},{8,9},{9,8},{10,11... | collective-permute-start | bytes 1179656 | tf_op jit(solution)/shard_map/ppermute | solution.py:388
  79.7 18.4 %copy-start.7 = (f32[32,128]{1,0:T(8,128)}, f32[32,128]{1,0:T(8,128)S(1)}, u32[]{:S(2)}) copy-start(f32[32,128]{1,0:T(8,128)S(1)} %get-tuple-element.35.diagonal_ref) | copy-start | bytes 49156
  79.8 18.4 %collective-permute-start.4 = (bf16[192,32,128]{2,1,0:T(8,128)(2,1)S(1)}, bf16[192,32,128]{2,1,0:T(8,128)(2,1)S(1)}, u32[]{:S(2)}, u32[]{:S(2)}) collective-permute-start(bf16[192,32,128]{2,1,0:T(8,128)(2,1)S(1)} %get-tuple-element.27), channel_id=1, source_target_pairs={{0,1},{1,0},{2,3},{3,2},{4,5},{5,4},{6,7},{7,6},{8,9},{9,8},{10,11... | collective-permute-start | bytes 4718600 | tf_op jit(solution)/shard_map/ppermute | solution.py:388
  96.4 1.7 %collective-permute-start.5 = (bf16[48,32,128]{2,1,0:T(8,128)(2,1)S(1)}, bf16[48,32,128]{2,1,0:T(8,128)(2,1)S(1)}, u32[]{:S(2)}, u32[]{:S(2)}) collective-permute-start(bf16[48,32,128]{2,1,0:T(8,128)(2,1)S(1)} %all_to_all.21.ghost_ref), channel_id=1, source_target_pairs={{0,1},{1,0},{2,3},{3,2},{4,5},{5,4},{6,7},{7,6},{8,9},{9,8},{10,11... | collective-permute-start | bytes 1179656 | tf_op jit(solution)/shard_map/ppermute | solution.py:388
  98.2 8.2 %copy-start.1 = (bf16[96,256,512]{2,1,0:T(8,128)(2,1)S(1)}, bf16[96,256,512]{2,1,0:T(8,128)(2,1)}, u32[]{:S(2)}) copy-start(bf16[96,256,512]{2,1,0:T(8,128)(2,1)} %copy-done) | copy-start | bytes 75497472
  127.3 0.6 copy-start.9
  127.9 21.8 %collective-permute-start.6 = (bf16[192,32,128]{2,1,0:T(8,128)(2,1)}, bf16[192,32,128]{2,1,0:T(8,128)(2,1)}, u32[]{:S(2)}, u32[]{:S(2)}) collective-permute-start(bf16[192,32,128]{2,1,0:T(8,128)(2,1)} %get-tuple-element.31), channel_id=1, source_target_pairs={{0,1},{1,0},{2,3},{3,2},{4,5},{5,4},{6,7},{7,6},{8,9},{9,8},{10,11... | collective-permute-start | bytes 4718600 | tf_op jit(solution)/shard_map/ppermute | solution.py:388
  128.1 3.6 %collective-permute-start.7 = (bf16[48,32,128]{2,1,0:T(8,128)(2,1)S(1)}, bf16[48,32,128]{2,1,0:T(8,128)(2,1)S(1)}, u32[]{:S(2)}, u32[]{:S(2)}) collective-permute-start(bf16[48,32,128]{2,1,0:T(8,128)(2,1)S(1)} %get-tuple-element.33), channel_id=1, source_target_pairs={{0,1},{1,0},{2,3},{3,2},{4,5},{5,4},{6,7},{7,6},{8,9},{9,8},{10,11... | collective-permute-start | bytes 1179656 | tf_op jit(solution)/shard_map/ppermute | solution.py:388
  132.1 0.8 copy-start.6
  132.8 16.9 %all-to-all-start.3 = ((bf16[48,32,128]{2,1,0:T(8,128)(2,1)}), bf16[48,32,128]{2,1,0:T(8,128)(2,1)S(1)}, u32[]{:S(2)}, u32[]{:S(2)}) async-start(bf16[48,32,128]{2,1,0:T(8,128)(2,1)} %copy-done.6), calls=%async_computation.3 | async-start | bytes 786432 | tf_op jit(solution)/shard_map/all_to_all | solution.py:391
  149.7 2.1 %copy-start.3 = (bf16[240,64,128]{2,1,0:T(8,128)(2,1)S(1)}, bf16[240,64,128]{2,1,0:T(8,128)(2,1)}, u32[]{:S(2)}) copy-start(bf16[240,64,128]{2,1,0:T(8,128)(2,1)} %copy-done.2) | copy-start | bytes 11796484
  151.9 0.7 copy-start.8
  152.6 0.7 copy-start.10
  153.3 0.7 copy-start.14

commit v2 on v1

v2 whole, which is shorter than its diff:
```python
import functools

import jax
import jax.numpy as jnp
from jax import lax
from jax.experimental import pallas as pl
from jax.experimental.pallas import tpu as pltpu
from jax.sharding import PartitionSpec as P

P_SIZE = 105
LANES = 128
MIB = 1 << 20
TOGETHER = 32

epsilon = 1e-06

f32 = jnp.float32
bf16 = jnp.bfloat16

VMEM = pl.BlockSpec(memory_space=pltpu.VMEM)
SMEM = pl.BlockSpec(memory_space=pltpu.SMEM)
ANY = pl.BlockSpec(memory_space=pl.ANY)
HBM = pl.BlockSpec(memory_space=pltpu.HBM)


def lane_ids(rows):
    return lax.broadcasted_iota(jnp.int32, (rows, LANES), 1)


def stat_lanes(columns):
    rows = columns[0].shape[0]
    lanes = lane_ids(rows)
    block = jnp.zeros((rows, LANES), f32)
    lane = P_SIZE
    for value in columns:
        rest = value * 0.5
        for _ in range(3):
            part = rest.astype(bf16).astype(f32)
            block = jnp.where(lanes == lane, part, block)
            rest = rest - part
            lane += 1
    return block


def read_stat(block, which):
    lanes = lane_ids(block.shape[0])
    first = P_SIZE + 3 * which
    inside = (lanes >= first) & (lanes < first + 3)
    return 2.0 * jnp.sum(jnp.where(inside, block, 0.0), axis=1, keepdims=True)


def gathered_block(ghost_ref, ranks):
    slots = ghost_ref.shape[0] // ranks
    total = ghost_ref[0].astype(f32)
    for rank in range(1, ranks):
        total = total + ghost_ref[rank * slots].astype(f32)
    return total


def first_payload_kernel(rhs_ref, send_ref, payload_ref):
    faces, rows, _ = rhs_ref.shape

    def add(face, total):
        value = rhs_ref[face].astype(f32)
        return total + value * value

    total = lax.fori_loop(0, faces, add, jnp.zeros((rows, P_SIZE), f32), unroll=8)
    stats = stat_lanes([jnp.sum(total, axis=1, keepdims=True)]).astype(bf16)

    @pl.loop(0, payload_ref.shape[0], unroll=4)
    def _(slot):
        payload_ref[slot] = stats
        payload_ref[slot, :, :P_SIZE] = rhs_ref[send_ref[0, slot]]


def relayout(source, perm_ref, tail_ref, target):
    group = source.shape[1]
    width = source.shape[2]
    full = P_SIZE // group
    rest = P_SIZE - full * group
    for slot in range(source.shape[0] // P_SIZE):
        for part in range(full + 1):
            first = slot * P_SIZE + part * group
            depth = group if part < full else rest
            chunk = source[first : first + depth].reshape(depth * group, width)
            perm = perm_ref[...] if part < full else tail_ref[...]
            moved = jnp.dot(perm, chunk, preferred_element_type=f32).astype(bf16)
            for element in range(group):
                target[element, pl.ds(slot * LANES + part * group, group), :width] = moved[
                    element * group : (element + 1) * group
                ]
        zeros = jnp.zeros((LANES - (full + 1) * group, target.shape[2]), bf16)
        for element in range(group):
            target[element, pl.ds(slot * LANES + (full + 1) * group, zeros.shape[0]), :] = zeros


def copy_group(source_ref, buffer, sems, step):
    group = buffer.shape[2]
    return pltpu.make_async_copy(
        source_ref.at[:, pl.ds(step * group, group), :], buffer.at[step % 2], sems.at[step % 2]
    )


def relayout_kernel(raw_ref, perm_ref, tail_ref, out_ref, buffer, staging, sems, out_sems):
    group = buffer.shape[2]
    steps = raw_ref.shape[1] // group

    def copy_out(step):
        return pltpu.make_async_copy(
            staging.at[step % 2], out_ref.at[pl.ds(step * group, group)], out_sems.at[step % 2]
        )

    copy_group(raw_ref, buffer, sems, 0).start()
    for step in range(steps):
        if step + 1 < steps:
            copy_group(raw_ref, buffer, sems, step + 1).start()
        copy_group(raw_ref, buffer, sems, step).wait()
        if step >= 2:
            copy_out(step - 2).wait()
        relayout(buffer.at[step % 2], perm_ref, tail_ref, staging.at[step % 2])
        copy_out(step).start()
    for step in range(max(0, steps - 2), steps):
        copy_out(step).wait()


def slot_pieces(terms):
    lanes = lane_ids(terms.shape[0])
    tiles = [terms[:, LANES * n : LANES * (n + 1)] for n in range(4)]
    pieces = [tiles[0]]
    for slot in range(1, 4):
        shift = slot * (LANES - P_SIZE)
        pieces.append(
            jnp.where(lanes < shift, pltpu.roll(tiles[slot - 1], shift, 1), pltpu.roll(tiles[slot], shift, 1))
        )
    return pieces


def add_terms(first, blocks, basis_ref, faces_ref, first_slot, sums_ref):
    pieces = []
    for inner, block in enumerate(blocks):
        left = basis_ref[faces_ref[first_slot, first + inner]]
        right = basis_ref[faces_ref[first_slot + 1, first + inner]]
        terms = jnp.dot(jnp.concatenate([left, right], axis=1), block(), preferred_element_type=f32)
        for slot, piece in enumerate(slot_pieces(terms)):
            pieces.append((faces_ref[slot, first + inner], piece))
    for slot, piece in pieces:
        sums_ref[slot] += piece


def held_apply(blocks_refs, *refs):
    first = 0
    for blocks_ref in blocks_refs:
        count = blocks_ref.shape[0]
        together = max(n for n in range(1, TOGETHER + 1) if count % n == 0)

        @pl.loop(0, count // together)
        def _(step, blocks_ref=blocks_ref, first=first, together=together):
            at = step * together
            add_terms(first + at, [lambda n=n: blocks_ref[at + n] for n in range(together)], *refs)

        first += count


def streamed_apply(blocks_ref, buffer, sems, *refs):
    group = buffer.shape[1]
    steps = blocks_ref.shape[0] // group

    def copy(step):
        return pltpu.make_async_copy(
            blocks_ref.at[pl.ds(step * group, group)], buffer.at[step % 2], sems.at[step % 2]
        )

    copy(0).start()
    for step in range(steps):
        if step + 1 < steps:
            copy(step + 1).start()
        copy(step).wait()
        add_terms(step * group, [lambda n=n: buffer[step % 2, n] for n in range(group)], *refs)


def relayout_apply(raw_ref, perm_ref, tail_ref, blocks_refs, buffer, sems, *refs):
    group = buffer.shape[2]
    targets = [
        (blocks_ref, first) for blocks_ref in blocks_refs for first in range(0, blocks_ref.shape[0], group)
    ]
    for step, (target, first) in enumerate(targets):
        copy_group(raw_ref, buffer, sems, step).wait()
        relayout(buffer.at[step % 2], perm_ref, tail_ref, target.at[pl.ds(first, group)])
        if step + 2 < len(targets):
            copy_group(raw_ref, buffer, sems, step + 2).start()
        add_terms(step * group, [lambda n=n: target[first + n] for n in range(group)], *refs)


def masked_sum(value):
    return jnp.sum(jnp.where(lane_ids(value.shape[0]) < P_SIZE, value, 0.0), axis=1, keepdims=True)


def slot_loop(first, last, step, carry):
    return lax.fori_loop(first, last, step, carry, unroll=4)


def ghost_lanes(sums_ref, stats, ghost_own_out, ghost_other_out):
    ghosts, half, _ = ghost_own_out.shape
    owned = sums_ref.shape[0] - ghosts
    inside = lane_ids(2 * half) < P_SIZE

    @pl.loop(0, ghosts, unroll=4)
    def _(slot):
        value = jnp.where(inside, sums_ref[owned + slot], stats).astype(bf16)
        ghost_own_out[slot] = value[:half]
        ghost_other_out[slot] = value[half:]


def norm_of(ghost_ref, ranks, entries):
    return jnp.sqrt(read_stat(gathered_block(ghost_ref, ranks), 0) / entries + epsilon)


def fill_ghosts(basis_ref, sums_ref, ghost_ref, ghost_other_ref, scale, scale_other):
    ghosts, half, _ = ghost_ref.shape
    owned = sums_ref.shape[0] - ghosts
    inside = lane_ids(half) < P_SIZE

    @pl.loop(0, ghosts, unroll=4)
    def _(slot):
        sums_ref[owned + slot] = jnp.zeros((2 * half, LANES), f32)
        basis_ref[owned + slot, :half] = jnp.where(inside, ghost_ref[slot].astype(f32) * scale, 0.0).astype(bf16)
        basis_ref[owned + slot, half:] = jnp.where(
            inside, ghost_other_ref[slot].astype(f32) * scale_other, 0.0
        ).astype(bf16)


def first_apply_kernel(
    ranks, entries, fused, rhs_ref, rhs_other_ref, ghost_ref, ghost_other_ref, faces_ref, *refs,
):
    owned, half, _ = rhs_ref.shape
    ghosts = ghost_ref.shape[0]
    rows = 2 * half
    if fused:
        raw_ref, perm_ref, tail_ref, *outs, buffer, sems = refs
        blocks_refs = outs[5:]
        for step in range(2):
            copy_group(raw_ref, buffer, sems, step).start()
    else:
        blocks_ref, *outs, buffer, sems = refs
    basis_ref, sums_ref, ghost_own_out, ghost_other_out, norm_ref = outs[:5]

    norm = norm_of(ghost_ref, ranks, entries)
    norm_ref[...] = jnp.broadcast_to(norm, (half, LANES))
    scale = 1.0 / norm
    scale_other = 1.0 / norm_of(ghost_other_ref, ranks, entries)

    @pl.loop(0, owned, unroll=4)
    def _(face):
        sums_ref[face] = jnp.zeros((rows, LANES), f32)
        basis_ref[face] = jnp.zeros((rows, LANES), bf16)
        basis_ref[face, :half, :P_SIZE] = (rhs_ref[face].astype(f32) * scale).astype(bf16)
        basis_ref[face, half:, :P_SIZE] = (rhs_other_ref[face].astype(f32) * scale_other).astype(bf16)

    fill_ghosts(basis_ref, sums_ref, ghost_ref, ghost_other_ref, scale, scale_other)
    field = (basis_ref, faces_ref, 2 * lax.axis_index("col"), sums_ref)
    if fused:
        relayout_apply(raw_ref, perm_ref, tail_ref, blocks_refs, buffer, sems, *field)
    else:
        streamed_apply(blocks_ref, buffer, sems, *field)

    def dot_step(slot, dot):
        return dot + basis_ref[slot].astype(f32) * sums_ref[slot]

    dot = slot_loop(0, owned + ghosts, dot_step, jnp.zeros((rows, LANES), f32))
    ghost_lanes(sums_ref, stat_lanes([masked_sum(dot)]), ghost_own_out, ghost_other_out)


def fields_kernel(sums_ref, own_ref, other_ref):
    owned, half, _ = own_ref.shape

    @pl.loop(0, owned, unroll=4)
    def _(slot):
        value = sums_ref[slot].astype(bf16)
        own_ref[slot] = value[:half]
        other_ref[slot] = value[half:]


def return_payload_kernel(stats, own_ref, other_ref, sums_ref, payload_ref, same_sums_ref):
    del sums_ref, same_sums_ref
    half = own_ref.shape[1]
    inside = lane_ids(half) < P_SIZE
    own = own_ref[0].astype(f32)
    other = other_ref[0].astype(f32)
    lanes = stat_lanes([read_stat(own, n) + read_stat(other, n) for n in range(stats)])

    @pl.loop(0, payload_ref.shape[0], unroll=4)
    def _(slot):
        total = own_ref[slot].astype(f32) + other_ref[slot].astype(f32)
        payload_ref[slot] = jnp.where(inside, total, lanes).astype(bf16)


def project_kernel(
    ranks, entries, own_ref, other_ref, returned_ref, basis_ref, send_ref,
    rounded_ref, payload_ref, diagonal_ref, projected_ref,
):
    owned, half, _ = own_ref.shape
    ghosts = payload_ref.shape[0]
    inside = lane_ids(half) < P_SIZE
    diagonal = read_stat(gathered_block(returned_ref, ranks), 0) / entries
    diagonal_ref[...] = jnp.broadcast_to(diagonal, (half, LANES))

    @pl.loop(0, owned, unroll=4)
    def _(face):
        projected_ref[face] = (
            own_ref[face].astype(f32)
            + other_ref[face].astype(f32)
            - diagonal * basis_ref[face, :half].astype(f32)
        )

    @pl.loop(0, ghosts)
    def _(slot):
        projected_ref[send_ref[0, slot]] += returned_ref[slot].astype(f32)

    def round_step(face, total):
        value = projected_ref[face]
        rounded_ref[face] = value.astype(bf16)
        return total + value * value

    total = slot_loop(0, owned, round_step, jnp.zeros((half, LANES), f32))
    stats = stat_lanes([masked_sum(total)]).astype(bf16)

    @pl.loop(0, ghosts, unroll=4)
    def _(slot):
        payload_ref[slot] = jnp.where(inside, rounded_ref[send_ref[0, slot]], stats)


def second_apply_kernel(
    ranks, entries, held, rounded_ref, rounded_other_ref, ghost_ref, ghost_other_ref, faces_ref, first_ref, spent_ref,
    *refs,
):
    del spent_ref
    stream = [] if held else refs[-2:]
    refs = refs if held else refs[:-2]
    *blocks_refs, basis_ref, sums_ref, ghost_own_out, ghost_other_out, norm_ref, second_ref, staging, out_sem = refs
    owned, half, _ = rounded_ref.shape
    ghosts = ghost_ref.shape[0]
    rows = 2 * half
    norm = norm_of(ghost_ref, ranks, entries)
    norm_ref[...] = jnp.broadcast_to(norm, (half, LANES))
    scale = 1.0 / norm
    scale_other = 1.0 / norm_of(ghost_other_ref, ranks, entries)

    @pl.loop(0, owned, unroll=4)
    def _(face):
        sums_ref[face] = jnp.zeros((rows, LANES), f32)
        value = (rounded_ref[face].astype(f32) * scale).astype(bf16)
        basis_ref[face, :half] = value
        staging[face] = value[:, :P_SIZE]
        basis_ref[face, half:] = (rounded_other_ref[face].astype(f32) * scale_other).astype(bf16)

    out_copy = pltpu.make_async_copy(staging, second_ref, out_sem)
    out_copy.start()
    fill_ghosts(basis_ref, sums_ref, ghost_ref, ghost_other_ref, scale, scale_other)
    field = (basis_ref, faces_ref, 2 * lax.axis_index("col"), sums_ref)
    if held:
        held_apply(blocks_refs, *field)
    else:
        streamed_apply(blocks_refs[0], *stream, *field)

    def dot_step(slot, dots):
        value = sums_ref[slot]
        return tuple(dot + basis[slot].astype(f32) * value for dot, basis in zip(dots, (first_ref, basis_ref)))

    zeros = jnp.zeros((rows, LANES), f32)
    dots = slot_loop(0, owned + ghosts, dot_step, (zeros, zeros))
    ghost_lanes(sums_ref, stat_lanes([masked_sum(dot) for dot in dots]), ghost_own_out, ghost_other_out)
    out_copy.wait()


def final_kernel(
    ranks, entries, own_ref, other_ref, returned_ref, first_ref, second_ref, send_ref, start_ref, diagonal_ref, next_ref,
    vector_ref, hessenberg_ref, image_ref,
):
    owned, half, _ = own_ref.shape
    block = gathered_block(returned_ref, ranks)
    proj_first = read_stat(block, 0) / entries
    proj_second = read_stat(block, 1) / entries

    @pl.loop(0, owned, unroll=4)
    def _(face):
        value = (
            own_ref[face].astype(f32)
            + other_ref[face].astype(f32)
            - proj_first * first_ref[face, :half].astype(f32)
        )
        image_ref[face] = value - proj_second * second_ref[face, :half].astype(f32)

    @pl.loop(0, returned_ref.shape[0])
    def _(slot):
        image_ref[send_ref[0, slot]] += returned_ref[slot].astype(f32)

    @pl.loop(0, owned, unroll=4)
    def _(face):
        vector_ref[face] = image_ref[face, :, :P_SIZE].astype(bf16)

    lanes = lane_ids(half)
    table = jnp.zeros((half, LANES), f32)
    for row, value in enumerate(
        [start_ref[...], diagonal_ref[...], next_ref[...], proj_first, proj_second]
    ):
        table = jnp.where(lanes == row, value, table)
    hessenberg_ref[...] = jnp.transpose(table)[: hessenberg_ref.shape[0]]


def call(kernel, out_shape, in_specs, scratch=(), limit=16, flops=0, bytes_accessed=0, **kwargs):
    return pl.pallas_call(
        kernel,
        out_shape=out_shape,
        in_specs=in_specs,
        scratch_shapes=scratch,
        compiler_params=pltpu.CompilerParams(vmem_limit_bytes=limit * MIB),
        cost_estimate=pl.CostEstimate(flops=flops, bytes_accessed=bytes_accessed, transcendentals=0),
        **kwargs,
    )


def body(adjoint_rhs, element_blocks, element_faces, send_faces):
    ranks = lax.axis_size("dom")
    rhs = jnp.transpose(adjoint_rhs, (0, 2, 1))
    owned, half, _ = rhs.shape
    entries = float(ranks * owned * P_SIZE)
    ghosts = send_faces.shape[1]
    elements, contracted, block_width = element_blocks.shape
    slots = owned + ghosts
    faces = element_faces.T
    raw = jnp.transpose(element_blocks, (1, 0, 2))
    group = 16
    rest = P_SIZE % group
    width = -(-block_width // LANES) * LANES
    sums_bytes = slots * 2 * half * LANES * 4
    resident = elements * 2 * LANES * width * 2 + 3 * sums_bytes <= 48 * MIB

    def out(shape, dtype=bf16):
        return pltpu.VMEM(shape, dtype) if resident else jax.ShapeDtypeStruct(shape, dtype)

    stream = [pltpu.VMEM((2, group, 2 * LANES, width), bf16), pltpu.SemaphoreType.DMA((2,))]

    def limit(amount):
        return amount if resident else 50

    def swap(value):
        return lax.ppermute(value, "col", [(0, 1), (1, 0)])

    def exchange(value):
        return lax.all_to_all(value, "dom", split_axis=0, concat_axis=0, tiled=True)

    rhs_other = swap(rhs)

    ghost_field = out((ghosts, half, LANES))
    payload = call(first_payload_kernel, ghost_field, [VMEM, SMEM], limit=limit(4))(rhs, send_faces)
    ghost = exchange(payload)

    row = jnp.arange(group * group)
    column = jnp.arange(group * group)
    perm = ((row[:, None] // group == column[None, :] % group) & (row[:, None] % group == column[None, :] // group))
    perm = perm.astype(bf16)
    tail = perm[:, : rest * group]
    raw_buffer = [pltpu.VMEM((2, contracted, group, block_width), bf16), pltpu.SemaphoreType.DMA((2,))]
    blocks_shape = (elements, 2 * LANES, width)
    parts = elements // (2 * group) if resident and elements % (2 * group) == 0 else 1
    if resident:
        operands = (raw, perm, tail)
    else:
        blocks = call(
            relayout_kernel,
            jax.ShapeDtypeStruct(blocks_shape, bf16),
            [HBM, VMEM, VMEM],
            [raw_buffer[0], stream[0], raw_buffer[1], stream[1]],
            limit=limit(20),
            out_specs=HBM,
        )(raw, perm, tail)
        operands = (blocks,)

    ghost_other = swap(ghost)

    field = out((owned, half, LANES))
    basis = out((slots, 2 * half, LANES))
    sums_field = out((slots, 2 * half, LANES), f32)
    column_values = out((half, LANES), f32)
    outs = (basis, sums_field, ghost_field, ghost_field, column_values)
    first_basis, sums, ghost_own, ghost_cross, start_norm, *blocks_held = call(
        functools.partial(first_apply_kernel, ranks, entries, resident),
        outs + ((out((elements // parts, *blocks_shape[1:])),) * parts if resident else ()),
        [VMEM] * 4 + [SMEM] + ([HBM, VMEM, VMEM] if resident else [HBM]),
        raw_buffer if resident else stream,
        limit=limit(12),
    )(rhs, rhs_other, ghost, ghost_other, faces, *operands)
    blocks = blocks_held if resident else [blocks]

    def return_payload(stats, ghost_own, ghost_cross, sums):
        return call(
            functools.partial(return_payload_kernel, stats), (ghost_field, sums_field),
            [VMEM, VMEM, ANY], limit=limit(4), input_output_aliases={2: 1}, out_specs=(VMEM, ANY),
        )(ghost_own, ghost_cross, sums)

    payload, sums = return_payload(1, ghost_own, swap(ghost_cross), sums)
    returned = exchange(payload)
    own, other = call(fields_kernel, (field, field), [VMEM], limit=limit(4))(sums)
    other = swap(other)

    rounded, payload, diagonal = call(
        functools.partial(project_kernel, ranks, entries),
        (field, ghost_field, column_values),
        [VMEM] * 4 + [SMEM],
        [pltpu.VMEM((owned, half, LANES), f32)],
        limit=limit(8),
    )(own, other, returned, first_basis, send_faces)

    rounded_other = swap(rounded)
    ghost = exchange(payload)
    ghost_other = swap(ghost)
    second_basis, sums, ghost_own, ghost_cross, next_norm, second = call(
        functools.partial(second_apply_kernel, ranks, entries, resident),
        outs + (jax.ShapeDtypeStruct((owned, half, P_SIZE), bf16),),
        [VMEM] * 4 + [SMEM, VMEM, ANY] + [VMEM if resident else HBM] * len(blocks),
        [pltpu.VMEM((owned, half, P_SIZE), bf16), pltpu.SemaphoreType.DMA] + ([] if resident else stream),
        limit=limit(6),
        out_specs=(VMEM,) * 5 + (HBM,),
        input_output_aliases={6: 1},
    )(rounded, rounded_other, ghost, ghost_other, faces, first_basis, sums, *blocks)

    payload, sums = return_payload(2, ghost_own, swap(ghost_cross), sums)
    returned = exchange(payload)
    own, other = call(fields_kernel, (field, field), [VMEM], limit=limit(4))(sums)
    other = swap(other)

    vector, hessenberg = call(
        functools.partial(final_kernel, ranks, entries),
        (jax.ShapeDtypeStruct((owned, half, P_SIZE), bf16), jax.ShapeDtypeStruct((5, half), f32)),
        [VMEM] * 5 + [SMEM] + [VMEM] * 3,
        [pltpu.VMEM((owned, half, LANES), f32)],
        limit=limit(10),
    )(own, other, returned, first_basis, second_basis, send_faces, start_norm, diagonal, next_norm)

    return (jnp.transpose(second, (0, 2, 1)), jnp.transpose(vector, (0, 2, 1)), hessenberg)


def solution(mesh):
    in_specs = (P("dom", None, "col"), P("dom", "col", None), P("dom", None), P("dom", None))
    out_specs = (P("dom", None, "col"), P("dom", None, "col"), P(None, "col"))
    return jax.shard_map(body, mesh=mesh, in_specs=in_specs, out_specs=out_specs, check_vma=False)
```

time: 161 us -> 122 us (0.76)
  blocking collectives: 33.2 us -> 71 us
  waiting for transfers between devices: 33.5 us -> 6.49 us
  Pallas kernels: 61.7 us -> 35.6 us
  starting transfers between devices: 13.3 us -> 1.31 us
  local copies, waits for them, and re-layouts: 16.9 us -> 6.67 us
    all_to_all x2 -> x4, blocking collectives: 33.2 us -> 71 us  [exchange(): return lax.all_to_all(value, 'dom', split_axis=0, concat_axis=0, tiled=True)]
    all_to_all x2 -> x0, waiting for transfers between devices: 25.1 us -> none  [exchange(): return lax.all_to_all(value, 'dom', split_axis=0, concat_axis=0, tiled=True)]
    pallas_call x7 -> x8, Pallas kernels: 55.9 us -> 31.9 us  [the longest x1 17.5 us: body(): call(functools.partial(first_apply_kernel, ranks, entries, resident), out...]
    all_to_all x2 -> x0, starting transfers between devices: 11.6 us -> none  [exchange(): return lax.all_to_all(value, 'dom', split_axis=0, concat_axis=0, tiled=True)]
    unnamed x31 -> x22, local copies, waits for them, and re-layouts: 16.9 us -> 6.67 us
    pallas_call x1, Pallas kernels: 5.81 us -> 3.75 us  [body(): call(functools.partial(final_kernel, ranks, entries), (jax.ShapeDtypeStru...]
    ppermute x8, waiting for transfers between devices: 8.48 us -> 6.49 us  [swap(): return lax.ppermute(value, 'col', [(0, 1), (1, 0)])]
  transfers between devices with their start and end apart: 10 -> 8, of which waited for: 5 -> 4; matrix products, arithmetic and copies ran while one was open for 1% -> 0% of each run, Pallas kernels for 9% -> 1%
where the time goes in v2:
time: 122 us
  blocking collectives  71 us (58%)
  Pallas kernels  35.6 us (29%)
  local copies, waits for them, and re-layouts  6.67 us (5%)
  waiting for transfers between devices  6.49 us (5%)
  starting transfers between devices  1.31 us (1%)
    all_to_all x4, blocking collectives, exchange(): return lax.all_to_all(value, 'dom', split_axis=0, concat_axis=0, tiled=True)  71 us
    pallas_call x1, Pallas kernels, body(): call(functools.partial(first_apply_kernel, ranks, entries, resident), out...  17.5 us
    pallas_call x1, Pallas kernels, body(): call(functools.partial(second_apply_kernel, ranks, entries, resident), ou...  9.24 us
    unnamed x22, local copies, waits for them, and re-layouts  6.67 us
    ppermute x8, waiting for transfers between devices, swap(): return lax.ppermute(value, 'col', [(0, 1), (1, 0)])  6.49 us
    pallas_call x1, Pallas kernels, body(): call(functools.partial(final_kernel, ranks, entries), (jax.ShapeDtypeStru...  3.75 us
    pallas_call x1, Pallas kernels, body(): call(functools.partial(project_kernel, ranks, entries), (field, ghost_fie...  2.57 us
  transfers between devices with their start and end apart: 8, of which 4 were waited for; matrix products, arithmetic and copies ran while one was open for 0% of the time, Pallas kernels for 1%

profile of v2, /device:TPU:0, one launch (start us, length us, event | category | flops | bytes accessed | tf_op | source)
XLA Modules:
  0.0 122.0 jit_solution(15192370873711138029)
XLA Ops:
  0.6 0.5 collective-permute-start
  1.1 1.4 %copy-done.2 = bf16[192,105,32]{1,2,0:T(8,128)(2,1)S(1)} copy-done((bf16[192,105,32]{1,2,0:T(8,128)(2,1)S(1)}, bf16[192,105,32]{1,2,0:T(8,128)(2,1)}, u32[]{:S(2)}) %copy-start.2) | copy-done | bytes 1290264
  2.6 0.7 copy-done.5
  3.2 1.2 shard_map.67
  4.4 20.8 %all_to_all.20.ghost_ref = bf16[48,32,128]{2,1,0:T(8,128)(2,1)S(1)} all-to-all(bf16[48,32,128]{2,1,0:T(8,128)(2,1)S(1)} %shard_map.67), channel_id=1, replica_groups=mesh['dom'=16,'col'=2] {'dom'}, dimensions={0} | all-to-all | bytes 786432 | tf_op jit(solution)/shard_map/all_to_all | solution.py:450
  25.2 0.0 collective-permute-start.1
  25.2 0.1 and_convert_fusion.refs_1_
  25.4 1.6 %collective-permute-done.1.ghost_other_ref = bf16[48,32,128]{2,1,0:T(8,128)(2,1)S(1)} collective-permute-done((bf16[48,32,128]{2,1,0:T(8,128)(2,1)S(1)}, bf16[48,32,128]{2,1,0:T(8,128)(2,1)S(1)}, u32[]{:S(2)}, u32[]{:S(2)}) %collective-permute-start.1) | collective-permute-done | bytes 393248 | tf_op jit(solution)/shard_map/ppermute | solution.py:447
  27.0 0.0 collective-permute-done.rhs_other_ref
  27.0 17.5 %shard_map.68 = (bf16[240,64,128]{2,1,0:T(8,128)(2,1)S(1)}, f32[240,64,128]{2,1,0:T(8,128)S(1)}, bf16[48,32,128]{2,1,0:T(8,128)(2,1)S(1)}, bf16[48,32,128]{2,1,0...) custom-call(bf16[192,32,105]{2,1,0:T(8,128)(2,1)S(1)} %bitcast.12, ...), custom_call_target="tpu_custom_call" | custom-call | tf_op jit(solution)/shard_map/pallas_call | solution.py:486
  44.5 3.2 %copy-done.1 = bf16[32,256,512]{2,1,0:T(8,128)(2,1)} copy-done((bf16[32,256,512]{2,1,0:T(8,128)(2,1)}, bf16[32,256,512]{2,1,0:T(8,128)(2,1)S(1)}, u32[]{:S(2)}) %copy-start.1) | copy-done | bytes 8388632
  47.7 0.1 collective-permute-start.2
  47.9 1.6 %collective-permute-done.2.other_ref = bf16[48,32,128]{2,1,0:T(8,128)(2,1)S(1)} collective-permute-done((bf16[48,32,128]{2,1,0:T(8,128)(2,1)S(1)}, bf16[48,32,128]{2,1,0:T(8,128)(2,1)S(1)}, u32[]{:S(2)}, u32[]{:S(2)}) %collective-permute-start.2) | collective-permute-done | bytes 393248 | tf_op jit(solution)/shard_map/ppermute | solution.py:447
  49.5 0.3 shard_map.69
  49.7 1.4 %copy-done = bf16[32,256,512]{2,1,0:T(8,128)(2,1)} copy-done((bf16[32,256,512]{2,1,0:T(8,128)(2,1)}, bf16[32,256,512]{2,1,0:T(8,128)(2,1)S(1)}, u32[]{:S(2)}) %copy-start) | copy-done | bytes 8388632
  51.1 0.4 shard_map.70
  51.5 0.2 collective-permute-start.3
  51.7 16.9 %all_to_all.21.returned_ref = bf16[48,32,128]{2,1,0:T(8,128)(2,1)S(1)} all-to-all(bf16[48,32,128]{2,1,0:T(8,128)(2,1)S(1)} %get-tuple-element.36), channel_id=1, replica_groups=mesh['dom'=16,'col'=2] {'dom'}, dimensions={0} | all-to-all | bytes 786432 | tf_op jit(solution)/shard_map/all_to_all | solution.py:450
  68.6 0.0 collective-permute-done.3.other_ref
  68.6 2.6 %shard_map.71 = (bf16[192,32,128]{2,1,0:T(8,128)(2,1)S(1)}, bf16[48,32,128]{2,1,0:T(8,128)(2,1)S(1)}, f32[32,128]{1,0:T(8,128)S(1)}) custom-call(bf16[192,32,128]{2,1,0:T(8,128)(2,1)S(1)} %get-tuple-element.34.own_ref, bf16[192,32,128]{2,1,0:T(8,128)(2,1)S(1)} %collective-permute-done.3.other_ref, bf16[48,32,128]{2,1,0:T(8,128)(2,1)S(1)} %all_to_all.21.returned_ref, ...), custom_call_target="tpu_custom_call" | custom-call | tf_op jit(solution)/shard_map/pallas_call | solution.py:506
  71.2 0.1 collective-permute-start.4
  71.3 16.6 %all_to_all.22.ghost_ref = bf16[48,32,128]{2,1,0:T(8,128)(2,1)S(1)} all-to-all(bf16[48,32,128]{2,1,0:T(8,128)(2,1)S(1)} %get-tuple-element.39), channel_id=1, replica_groups=mesh['dom'=16,'col'=2] {'dom'}, dimensions={0} | all-to-all | bytes 786432 | tf_op jit(solution)/shard_map/all_to_all | solution.py:450
  87.9 0.0 collective-permute-start.5
  87.9 1.7 %collective-permute-done.5.ghost_other_ref = bf16[48,32,128]{2,1,0:T(8,128)(2,1)S(1)} collective-permute-done((bf16[48,32,128]{2,1,0:T(8,128)(2,1)S(1)}, bf16[48,32,128]{2,1,0:T(8,128)(2,1)S(1)}, u32[]{:S(2)}, u32[]{:S(2)}) %collective-permute-start.5) | collective-permute-done | bytes 393248 | tf_op jit(solution)/shard_map/ppermute | solution.py:447
  89.7 9.2 %shard_map.72 = (bf16[240,64,128]{2,1,0:T(8,128)(2,1)S(1)}, f32[240,64,128]{2,1,0:T(8,128)S(1)}, bf16[48,32,128]{2,1,0:T(8,128)(2,1)S(1)}, bf16[48,32,128]{2,1,0...) custom-call(bf16[192,32,128]{2,1,0:T(8,128)(2,1)S(1)} %get-tuple-element, ...), custom_call_target="tpu_custom_call", output_to_operand_aliasing={{1}: (6, {})} | custom-call | tf_op jit(solution)/shard_map/pallas_call | solution.py:517
  98.9 0.2 collective-permute-start.6
  99.1 1.6 %collective-permute-done.6.other_ref = bf16[48,32,128]{2,1,0:T(8,128)(2,1)S(1)} collective-permute-done((bf16[48,32,128]{2,1,0:T(8,128)(2,1)S(1)}, bf16[48,32,128]{2,1,0:T(8,128)(2,1)S(1)}, u32[]{:S(2)}, u32[]{:S(2)}) %collective-permute-start.6) | collective-permute-done | bytes 393248 | tf_op jit(solution)/shard_map/ppermute | solution.py:447
  100.7 0.3 shard_map.73
  101.0 0.4 shard_map.74
  101.4 0.2 collective-permute-start.7
  101.6 16.6 %all_to_all.23.returned_ref = bf16[48,32,128]{2,1,0:T(8,128)(2,1)S(1)} all-to-all(bf16[48,32,128]{2,1,0:T(8,128)(2,1)S(1)} %get-tuple-element.50), channel_id=1, replica_groups=mesh['dom'=16,'col'=2] {'dom'}, dimensions={0} | all-to-all | bytes 786432 | tf_op jit(solution)/shard_map/all_to_all | solution.py:450
  118.2 3.8 %shard_map.75 = (bf16[192,32,105]{2,1,0:T(8,128)(2,1)}, f32[5,32]{1,0:T(8,128)}) custom-call(bf16[192,32,128]{2,1,0:T(8,128)(2,1)S(1)} %get-tuple-element.48.own_ref, bf16[192,32,128]{2,1,0:T(8,128)(2,1)S(1)} %collective-permute-done.7.other_ref, bf16[48,32,128]{2,1,0:T(8,128)(2,1)S(1)} %all_to_all.23.returned_ref, ...), custom_call_target="tpu_custom_call" | custom-call | tf_op jit(solution)/shard_map/pallas_call | solution.py:532
  (23 shorter events, 0.0 us)
Async XLA Ops:
  0.6 26.3 %collective-permute-start = (bf16[192,32,105]{2,1,0:T(8,128)(2,1)}, bf16[192,32,105]{2,1,0:T(8,128)(2,1)S(1)}, u32[]{:S(2)}, u32[]{:S(2)}) collective-permute-start(bf16[192,32,105]{2,1,0:T(8,128)(2,1)} %bitcast.10), channel_id=1, source_target_pairs={{0,1},{1,0},{2,3},{3,2},{4,5},{5,4},{6,7},{7,6},{8,9},{9,8},{10,11... | collective-permute-start | bytes 3870728 | tf_op jit(solution)/shard_map/ppermute | solution.py:447
  1.1 1.4 %copy-start.2 = (bf16[192,105,32]{1,2,0:T(8,128)(2,1)S(1)}, bf16[192,105,32]{1,2,0:T(8,128)(2,1)}, u32[]{:S(2)}) copy-start(bf16[192,105,32]{1,2,0:T(8,128)(2,1)} %param.4) | copy-start | bytes 3870724
  2.6 0.7 copy-start.5
  3.2 23.7 %copy-start.3 = (bf16[192,105,32]{1,2,0:T(8,128)(2,1)S(1)}, bf16[192,105,32]{1,2,0:T(8,128)(2,1)}, u32[]{:S(2)}) copy-start(bf16[192,105,32]{1,2,0:T(8,128)(2,1)} %param.4) | copy-start | bytes 3870724
  3.2 23.7 %copy-start.4 = (s32[96,4]{0,1:T(4,128)S(1)}, s32[96,4]{0,1:T(4,128)}, u32[]{:S(2)}) copy-start(s32[96,4]{0,1:T(4,128)} %param.6) | copy-start | bytes 4612
  25.2 1.7 %collective-permute-start.1 = (bf16[48,32,128]{2,1,0:T(8,128)(2,1)S(1)}, bf16[48,32,128]{2,1,0:T(8,128)(2,1)S(1)}, u32[]{:S(2)}, u32[]{:S(2)}) collective-permute-start(bf16[48,32,128]{2,1,0:T(8,128)(2,1)S(1)} %all_to_all.20.ghost_ref), channel_id=1, source_target_pairs={{0,1},{1,0},{2,3},{3,2},{4,5},{5,4},{6,7},{7,6},{8,9},{9,8},{10,11... | collective-permute-start | bytes 1179656 | tf_op jit(solution)/shard_map/ppermute | solution.py:447
  44.5 3.2 %copy-start.1 = (bf16[32,256,512]{2,1,0:T(8,128)(2,1)}, bf16[32,256,512]{2,1,0:T(8,128)(2,1)S(1)}, u32[]{:S(2)}) copy-start(bf16[32,256,512]{2,1,0:T(8,128)(2,1)S(1)} %get-tuple-element.42.refs_2_) | copy-start | bytes 25165828
  47.7 3.4 %copy-start = (bf16[32,256,512]{2,1,0:T(8,128)(2,1)}, bf16[32,256,512]{2,1,0:T(8,128)(2,1)S(1)}, u32[]{:S(2)}) copy-start(bf16[32,256,512]{2,1,0:T(8,128)(2,1)S(1)} %get-tuple-element.41.refs_1_) | copy-start | bytes 25165828
  47.7 1.7 %collective-permute-start.2 = (bf16[48,32,128]{2,1,0:T(8,128)(2,1)S(1)}, bf16[48,32,128]{2,1,0:T(8,128)(2,1)S(1)}, u32[]{:S(2)}, u32[]{:S(2)}) collective-permute-start(bf16[48,32,128]{2,1,0:T(8,128)(2,1)S(1)} %get-tuple-element.31), channel_id=1, source_target_pairs={{0,1},{1,0},{2,3},{3,2},{4,5},{5,4},{6,7},{7,6},{8,9},{9,8},{10,11... | collective-permute-start | bytes 1179656 | tf_op jit(solution)/shard_map/ppermute | solution.py:447
  49.5 40.2 %slice-start.2 = ((s8[8388608]{0:T(1024)(128)(4,1)}), s8[4194304]{0:T(1024)(128)(4,1)S(1)}, s32[]{:S(2)}) async-start(s8[8388608]{0:T(1024)(128)(4,1)} %bitcast.8), calls=%async_computation.6 | async-start | bytes 8388608
  51.1 17.5 %copy-start.6 = (s32[1,48]{1,0:T(1,128)S(1)}, s32[1,48]{1,0:T(1,128)}, u32[]{:S(2)}) copy-start(s32[1,48]{1,0:T(1,128)} %send_ref.5) | copy-start | bytes 580
  51.1 38.5 %slice-start = ((s8[8388608]{0:T(1024)(128)(4,1)}), s8[4194304]{0:T(1024)(128)(4,1)S(1)}, s32[]{:S(2)}) async-start(s8[8388608]{0:T(1024)(128)(4,1)} %bitcast.6), calls=%async_computation.4 | async-start | bytes 8388608
  51.1 38.5 %slice-start.3 = ((s8[8388608]{0:T(1024)(128)(4,1)}), s8[4194304]{0:T(1024)(128)(4,1)S(1)}, s32[]{:S(2)}) async-start(s8[8388608]{0:T(1024)(128)(4,1)} %bitcast.8), calls=%async_computation.7 | async-start | bytes 8388608
  51.5 17.1 %collective-permute-start.3 = (bf16[192,32,128]{2,1,0:T(8,128)(2,1)S(1)}, bf16[192,32,128]{2,1,0:T(8,128)(2,1)S(1)}, u32[]{:S(2)}, u32[]{:S(2)}) collective-permute-start(bf16[192,32,128]{2,1,0:T(8,128)(2,1)S(1)} %get-tuple-element.35), channel_id=1, source_target_pairs={{0,1},{1,0},{2,3},{3,2},{4,5},{5,4},{6,7},{7,6},{8,9},{9,8},{10,11... | collective-permute-start | bytes 4718600 | tf_op jit(solution)/shard_map/ppermute | solution.py:447
  51.7 37.9 %slice-start.1 = ((s8[8388608]{0:T(1024)(128)(4,1)}), s8[4194304]{0:T(1024)(128)(4,1)S(1)}, s32[]{:S(2)}) async-start(s8[8388608]{0:T(1024)(128)(4,1)} %bitcast.6), calls=%async_computation.5 | async-start | bytes 8388608
  71.2 18.4 %collective-permute-start.4 = (bf16[192,32,128]{2,1,0:T(8,128)(2,1)S(1)}, bf16[192,32,128]{2,1,0:T(8,128)(2,1)S(1)}, u32[]{:S(2)}, u32[]{:S(2)}) collective-permute-start(bf16[192,32,128]{2,1,0:T(8,128)(2,1)S(1)} %get-tuple-element.38.rounded_ref), channel_id=1, source_target_pairs={{0,1},{1,0},{2,3},{3,2},{4,5},{5,4},{6,7},{7,6},{8,9},{9,8},{10,11... | collective-permute-start | bytes 4718600 | tf_op jit(solution)/shard_map/ppermute | solution.py:447
  87.9 1.7 %collective-permute-start.5 = (bf16[48,32,128]{2,1,0:T(8,128)(2,1)S(1)}, bf16[48,32,128]{2,1,0:T(8,128)(2,1)S(1)}, u32[]{:S(2)}, u32[]{:S(2)}) collective-permute-start(bf16[48,32,128]{2,1,0:T(8,128)(2,1)S(1)} %all_to_all.22.ghost_ref), channel_id=1, source_target_pairs={{0,1},{1,0},{2,3},{3,2},{4,5},{5,4},{6,7},{7,6},{8,9},{9,8},{10,11... | collective-permute-start | bytes 1179656 | tf_op jit(solution)/shard_map/ppermute | solution.py:447
  98.9 1.8 %collective-permute-start.6 = (bf16[48,32,128]{2,1,0:T(8,128)(2,1)S(1)}, bf16[48,32,128]{2,1,0:T(8,128)(2,1)S(1)}, u32[]{:S(2)}, u32[]{:S(2)}) collective-permute-start(bf16[48,32,128]{2,1,0:T(8,128)(2,1)S(1)} %get-tuple-element.45), channel_id=1, source_target_pairs={{0,1},{1,0},{2,3},{3,2},{4,5},{5,4},{6,7},{7,6},{8,9},{9,8},{10,11... | collective-permute-start | bytes 1179656 | tf_op jit(solution)/shard_map/ppermute | solution.py:447
  101.4 16.8 %collective-permute-start.7 = (bf16[192,32,128]{2,1,0:T(8,128)(2,1)S(1)}, bf16[192,32,128]{2,1,0:T(8,128)(2,1)S(1)}, u32[]{:S(2)}, u32[]{:S(2)}) collective-permute-start(bf16[192,32,128]{2,1,0:T(8,128)(2,1)S(1)} %get-tuple-element.49), channel_id=1, source_target_pairs={{0,1},{1,0},{2,3},{3,2},{4,5},{5,4},{6,7},{7,6},{8,9},{9,8},{10,11... | collective-permute-start | bytes 4718600 | tf_op jit(solution)/shard_map/ppermute | solution.py:447

commit v3 on v2

--- a/solution.py
+++ b/solution.py
@@ -183,12 +183,18 @@
     targets = [
         (blocks_ref, first) for blocks_ref in blocks_refs for first in range(0, blocks_ref.shape[0], group)
     ]
+    def apply_step(step):
+        target, first = targets[step]
+        add_terms(step * group, [lambda n=n: target[first + n] for n in range(group)], *refs)
+
     for step, (target, first) in enumerate(targets):
         copy_group(raw_ref, buffer, sems, step).wait()
         relayout(buffer.at[step % 2], perm_ref, tail_ref, target.at[pl.ds(first, group)])
+        if step:
+            apply_step(step - 1)
         if step + 2 < len(targets):
             copy_group(raw_ref, buffer, sems, step + 2).start()
-        add_terms(step * group, [lambda n=n: target[first + n] for n in range(group)], *refs)
+    apply_step(len(targets) - 1)
 
 
 def masked_sum(value):

time: 122 us -> 121 us (level)
  no operation moved by 1% of the time
where the time goes in v3:
time: 121 us
  blocking collectives  71 us (59%)
  Pallas kernels  34.9 us (29%)
  local copies, waits for them, and re-layouts  6.49 us (5%)
  waiting for transfers between devices  6.49 us (5%)
  starting transfers between devices  1.31 us (1%)
    all_to_all x4, blocking collectives, exchange(): return lax.all_to_all(value, 'dom', split_axis=0, concat_axis=0, tiled=True)  71 us
    pallas_call x1, Pallas kernels, body(): call(functools.partial(first_apply_kernel, ranks, entries, resident), out...  16.6 us
    pallas_call x1, Pallas kernels, body(): call(functools.partial(second_apply_kernel, ranks, entries, resident), ou...  9.24 us
    unnamed x22, local copies, waits for them, and re-layouts  6.49 us
    ppermute x8, waiting for transfers between devices, swap(): return lax.ppermute(value, 'col', [(0, 1), (1, 0)])  6.49 us
    pallas_call x1, Pallas kernels, body(): call(functools.partial(final_kernel, ranks, entries), (jax.ShapeDtypeStru...  3.75 us
    pallas_call x1, Pallas kernels, body(): call(functools.partial(project_kernel, ranks, entries), (field, ghost_fie...  2.57 us
  transfers between devices with their start and end apart: 8, of which 4 were waited for; matrix products, arithmetic and copies ran while one was open for 0% of the time, Pallas kernels for 1%

profile of v3, /device:TPU:0, one launch (start us, length us, event | category | flops | bytes accessed | tf_op | source)
XLA Modules:
  0.0 121.1 jit_solution(7212990099409649993)
XLA Ops:
  0.6 0.5 collective-permute-start
  1.1 1.4 %copy-done.2 = bf16[192,105,32]{1,2,0:T(8,128)(2,1)S(1)} copy-done((bf16[192,105,32]{1,2,0:T(8,128)(2,1)S(1)}, bf16[192,105,32]{1,2,0:T(8,128)(2,1)}, u32[]{:S(2)}) %copy-start.2) | copy-done | bytes 1290264
  2.6 0.7 copy-done.5
  3.2 1.2 shard_map.67
  4.4 20.8 %all_to_all.20.ghost_ref = bf16[48,32,128]{2,1,0:T(8,128)(2,1)S(1)} all-to-all(bf16[48,32,128]{2,1,0:T(8,128)(2,1)S(1)} %shard_map.67), channel_id=1, replica_groups=mesh['dom'=16,'col'=2] {'dom'}, dimensions={0} | all-to-all | bytes 786432 | tf_op jit(solution)/shard_map/all_to_all | solution.py:456
  25.2 0.0 collective-permute-start.1
  25.2 0.1 and_convert_fusion.refs_1_
  25.4 1.6 %collective-permute-done.1.ghost_other_ref = bf16[48,32,128]{2,1,0:T(8,128)(2,1)S(1)} collective-permute-done((bf16[48,32,128]{2,1,0:T(8,128)(2,1)S(1)}, bf16[48,32,128]{2,1,0:T(8,128)(2,1)S(1)}, u32[]{:S(2)}, u32[]{:S(2)}) %collective-permute-start.1) | collective-permute-done | bytes 393248 | tf_op jit(solution)/shard_map/ppermute | solution.py:453
  27.0 0.0 collective-permute-done.rhs_other_ref
  27.0 16.6 %shard_map.68 = (bf16[240,64,128]{2,1,0:T(8,128)(2,1)S(1)}, f32[240,64,128]{2,1,0:T(8,128)S(1)}, bf16[48,32,128]{2,1,0:T(8,128)(2,1)S(1)}, bf16[48,32,128]{2,1,0...) custom-call(bf16[192,32,105]{2,1,0:T(8,128)(2,1)S(1)} %bitcast.12, ...), custom_call_target="tpu_custom_call" | custom-call | tf_op jit(solution)/shard_map/pallas_call | solution.py:492
  43.6 3.2 %copy-done.1 = bf16[32,256,512]{2,1,0:T(8,128)(2,1)} copy-done((bf16[32,256,512]{2,1,0:T(8,128)(2,1)}, bf16[32,256,512]{2,1,0:T(8,128)(2,1)S(1)}, u32[]{:S(2)}) %copy-start.1) | copy-done | bytes 8388632
  46.8 0.1 collective-permute-start.2
  46.9 1.6 %collective-permute-done.2.other_ref = bf16[48,32,128]{2,1,0:T(8,128)(2,1)S(1)} collective-permute-done((bf16[48,32,128]{2,1,0:T(8,128)(2,1)S(1)}, bf16[48,32,128]{2,1,0:T(8,128)(2,1)S(1)}, u32[]{:S(2)}, u32[]{:S(2)}) %collective-permute-start.2) | collective-permute-done | bytes 393248 | tf_op jit(solution)/shard_map/ppermute | solution.py:453
  48.5 0.4 shard_map.69
  49.0 1.2 copy-done
  50.2 0.4 shard_map.70
  50.6 0.2 collective-permute-start.3
  50.8 16.9 %all_to_all.21.returned_ref = bf16[48,32,128]{2,1,0:T(8,128)(2,1)S(1)} all-to-all(bf16[48,32,128]{2,1,0:T(8,128)(2,1)S(1)} %get-tuple-element.36), channel_id=1, replica_groups=mesh['dom'=16,'col'=2] {'dom'}, dimensions={0} | all-to-all | bytes 786432 | tf_op jit(solution)/shard_map/all_to_all | solution.py:456
  67.7 0.0 collective-permute-done.3.other_ref
  67.7 2.6 %shard_map.71 = (bf16[192,32,128]{2,1,0:T(8,128)(2,1)S(1)}, bf16[48,32,128]{2,1,0:T(8,128)(2,1)S(1)}, f32[32,128]{1,0:T(8,128)S(1)}) custom-call(bf16[192,32,128]{2,1,0:T(8,128)(2,1)S(1)} %get-tuple-element.34.own_ref, bf16[192,32,128]{2,1,0:T(8,128)(2,1)S(1)} %collective-permute-done.3.other_ref, bf16[48,32,128]{2,1,0:T(8,128)(2,1)S(1)} %all_to_all.21.returned_ref, ...), custom_call_target="tpu_custom_call" | custom-call | tf_op jit(solution)/shard_map/pallas_call | solution.py:512
  70.3 0.1 collective-permute-start.4
  70.4 16.6 %all_to_all.22.ghost_ref = bf16[48,32,128]{2,1,0:T(8,128)(2,1)S(1)} all-to-all(bf16[48,32,128]{2,1,0:T(8,128)(2,1)S(1)} %get-tuple-element.39), channel_id=1, replica_groups=mesh['dom'=16,'col'=2] {'dom'}, dimensions={0} | all-to-all | bytes 786432 | tf_op jit(solution)/shard_map/all_to_all | solution.py:456
  87.0 0.0 collective-permute-start.5
  87.0 1.7 %collective-permute-done.5.ghost_other_ref = bf16[48,32,128]{2,1,0:T(8,128)(2,1)S(1)} collective-permute-done((bf16[48,32,128]{2,1,0:T(8,128)(2,1)S(1)}, bf16[48,32,128]{2,1,0:T(8,128)(2,1)S(1)}, u32[]{:S(2)}, u32[]{:S(2)}) %collective-permute-start.5) | collective-permute-done | bytes 393248 | tf_op jit(solution)/shard_map/ppermute | solution.py:453
  88.8 9.2 %shard_map.72 = (bf16[240,64,128]{2,1,0:T(8,128)(2,1)S(1)}, f32[240,64,128]{2,1,0:T(8,128)S(1)}, bf16[48,32,128]{2,1,0:T(8,128)(2,1)S(1)}, bf16[48,32,128]{2,1,0...) custom-call(bf16[192,32,128]{2,1,0:T(8,128)(2,1)S(1)} %get-tuple-element, ...), custom_call_target="tpu_custom_call", output_to_operand_aliasing={{1}: (6, {})} | custom-call | tf_op jit(solution)/shard_map/pallas_call | solution.py:523
  98.0 0.2 collective-permute-start.6
  98.2 1.6 %collective-permute-done.6.other_ref = bf16[48,32,128]{2,1,0:T(8,128)(2,1)S(1)} collective-permute-done((bf16[48,32,128]{2,1,0:T(8,128)(2,1)S(1)}, bf16[48,32,128]{2,1,0:T(8,128)(2,1)S(1)}, u32[]{:S(2)}, u32[]{:S(2)}) %collective-permute-start.6) | collective-permute-done | bytes 393248 | tf_op jit(solution)/shard_map/ppermute | solution.py:453
  99.8 0.3 shard_map.73
  100.1 0.4 shard_map.74
  100.5 0.2 collective-permute-start.7
  100.7 16.6 %all_to_all.23.returned_ref = bf16[48,32,128]{2,1,0:T(8,128)(2,1)S(1)} all-to-all(bf16[48,32,128]{2,1,0:T(8,128)(2,1)S(1)} %get-tuple-element.50), channel_id=1, replica_groups=mesh['dom'=16,'col'=2] {'dom'}, dimensions={0} | all-to-all | bytes 786432 | tf_op jit(solution)/shard_map/all_to_all | solution.py:456
  117.3 3.8 %shard_map.75 = (bf16[192,32,105]{2,1,0:T(8,128)(2,1)}, f32[5,32]{1,0:T(8,128)}) custom-call(bf16[192,32,128]{2,1,0:T(8,128)(2,1)S(1)} %get-tuple-element.48.own_ref, bf16[192,32,128]{2,1,0:T(8,128)(2,1)S(1)} %collective-permute-done.7.other_ref, bf16[48,32,128]{2,1,0:T(8,128)(2,1)S(1)} %all_to_all.23.returned_ref, ...), custom_call_target="tpu_custom_call" | custom-call | tf_op jit(solution)/shard_map/pallas_call | solution.py:538
  (23 shorter events, 0.0 us)
Async XLA Ops:
  0.6 26.3 %collective-permute-start = (bf16[192,32,105]{2,1,0:T(8,128)(2,1)}, bf16[192,32,105]{2,1,0:T(8,128)(2,1)S(1)}, u32[]{:S(2)}, u32[]{:S(2)}) collective-permute-start(bf16[192,32,105]{2,1,0:T(8,128)(2,1)} %bitcast.10), channel_id=1, source_target_pairs={{0,1},{1,0},{2,3},{3,2},{4,5},{5,4},{6,7},{7,6},{8,9},{9,8},{10,11... | collective-permute-start | bytes 3870728 | tf_op jit(solution)/shard_map/ppermute | solution.py:453
  1.1 1.4 %copy-start.2 = (bf16[192,105,32]{1,2,0:T(8,128)(2,1)S(1)}, bf16[192,105,32]{1,2,0:T(8,128)(2,1)}, u32[]{:S(2)}) copy-start(bf16[192,105,32]{1,2,0:T(8,128)(2,1)} %param.4) | copy-start | bytes 3870724
  2.6 0.7 copy-start.5
  3.2 23.7 %copy-start.3 = (bf16[192,105,32]{1,2,0:T(8,128)(2,1)S(1)}, bf16[192,105,32]{1,2,0:T(8,128)(2,1)}, u32[]{:S(2)}) copy-start(bf16[192,105,32]{1,2,0:T(8,128)(2,1)} %param.4) | copy-start | bytes 3870724
  3.2 23.7 %copy-start.4 = (s32[96,4]{0,1:T(4,128)S(1)}, s32[96,4]{0,1:T(4,128)}, u32[]{:S(2)}) copy-start(s32[96,4]{0,1:T(4,128)} %param.6) | copy-start | bytes 4612
  25.2 1.7 %collective-permute-start.1 = (bf16[48,32,128]{2,1,0:T(8,128)(2,1)S(1)}, bf16[48,32,128]{2,1,0:T(8,128)(2,1)S(1)}, u32[]{:S(2)}, u32[]{:S(2)}) collective-permute-start(bf16[48,32,128]{2,1,0:T(8,128)(2,1)S(1)} %all_to_all.20.ghost_ref), channel_id=1, source_target_pairs={{0,1},{1,0},{2,3},{3,2},{4,5},{5,4},{6,7},{7,6},{8,9},{9,8},{10,11... | collective-permute-start | bytes 1179656 | tf_op jit(solution)/shard_map/ppermute | solution.py:453
  43.6 3.2 %copy-start.1 = (bf16[32,256,512]{2,1,0:T(8,128)(2,1)}, bf16[32,256,512]{2,1,0:T(8,128)(2,1)S(1)}, u32[]{:S(2)}) copy-start(bf16[32,256,512]{2,1,0:T(8,128)(2,1)S(1)} %get-tuple-element.42.refs_2_) | copy-start | bytes 25165828
  46.8 3.4 %copy-start = (bf16[32,256,512]{2,1,0:T(8,128)(2,1)}, bf16[32,256,512]{2,1,0:T(8,128)(2,1)S(1)}, u32[]{:S(2)}) copy-start(bf16[32,256,512]{2,1,0:T(8,128)(2,1)S(1)} %get-tuple-element.41.refs_1_) | copy-start | bytes 25165828
  46.8 1.7 %collective-permute-start.2 = (bf16[48,32,128]{2,1,0:T(8,128)(2,1)S(1)}, bf16[48,32,128]{2,1,0:T(8,128)(2,1)S(1)}, u32[]{:S(2)}, u32[]{:S(2)}) collective-permute-start(bf16[48,32,128]{2,1,0:T(8,128)(2,1)S(1)} %get-tuple-element.31), channel_id=1, source_target_pairs={{0,1},{1,0},{2,3},{3,2},{4,5},{5,4},{6,7},{7,6},{8,9},{9,8},{10,11... | collective-permute-start | bytes 1179656 | tf_op jit(solution)/shard_map/ppermute | solution.py:453
  48.5 40.2 %slice-start.2 = ((s8[8388608]{0:T(1024)(128)(4,1)}), s8[4194304]{0:T(1024)(128)(4,1)S(1)}, s32[]{:S(2)}) async-start(s8[8388608]{0:T(1024)(128)(4,1)} %bitcast.8), calls=%async_computation.6 | async-start | bytes 8388608
  50.2 17.6 %copy-start.6 = (s32[1,48]{1,0:T(1,128)S(1)}, s32[1,48]{1,0:T(1,128)}, u32[]{:S(2)}) copy-start(s32[1,48]{1,0:T(1,128)} %send_ref.5) | copy-start | bytes 580
  50.2 38.6 %slice-start = ((s8[8388608]{0:T(1024)(128)(4,1)}), s8[4194304]{0:T(1024)(128)(4,1)S(1)}, s32[]{:S(2)}) async-start(s8[8388608]{0:T(1024)(128)(4,1)} %bitcast.6), calls=%async_computation.4 | async-start | bytes 8388608
  50.2 38.6 %slice-start.3 = ((s8[8388608]{0:T(1024)(128)(4,1)}), s8[4194304]{0:T(1024)(128)(4,1)S(1)}, s32[]{:S(2)}) async-start(s8[8388608]{0:T(1024)(128)(4,1)} %bitcast.8), calls=%async_computation.7 | async-start | bytes 8388608
  50.6 17.1 %collective-permute-start.3 = (bf16[192,32,128]{2,1,0:T(8,128)(2,1)S(1)}, bf16[192,32,128]{2,1,0:T(8,128)(2,1)S(1)}, u32[]{:S(2)}, u32[]{:S(2)}) collective-permute-start(bf16[192,32,128]{2,1,0:T(8,128)(2,1)S(1)} %get-tuple-element.35), channel_id=1, source_target_pairs={{0,1},{1,0},{2,3},{3,2},{4,5},{5,4},{6,7},{7,6},{8,9},{9,8},{10,11... | collective-permute-start | bytes 4718600 | tf_op jit(solution)/shard_map/ppermute | solution.py:453
  50.8 38.0 %slice-start.1 = ((s8[8388608]{0:T(1024)(128)(4,1)}), s8[4194304]{0:T(1024)(128)(4,1)S(1)}, s32[]{:S(2)}) async-start(s8[8388608]{0:T(1024)(128)(4,1)} %bitcast.6), calls=%async_computation.5 | async-start | bytes 8388608
  70.3 18.4 %collective-permute-start.4 = (bf16[192,32,128]{2,1,0:T(8,128)(2,1)S(1)}, bf16[192,32,128]{2,1,0:T(8,128)(2,1)S(1)}, u32[]{:S(2)}, u32[]{:S(2)}) collective-permute-start(bf16[192,32,128]{2,1,0:T(8,128)(2,1)S(1)} %get-tuple-element.38.rounded_ref), channel_id=1, source_target_pairs={{0,1},{1,0},{2,3},{3,2},{4,5},{5,4},{6,7},{7,6},{8,9},{9,8},{10,11... | collective-permute-start | bytes 4718600 | tf_op jit(solution)/shard_map/ppermute | solution.py:453
  87.0 1.7 %collective-permute-start.5 = (bf16[48,32,128]{2,1,0:T(8,128)(2,1)S(1)}, bf16[48,32,128]{2,1,0:T(8,128)(2,1)S(1)}, u32[]{:S(2)}, u32[]{:S(2)}) collective-permute-start(bf16[48,32,128]{2,1,0:T(8,128)(2,1)S(1)} %all_to_all.22.ghost_ref), channel_id=1, source_target_pairs={{0,1},{1,0},{2,3},{3,2},{4,5},{5,4},{6,7},{7,6},{8,9},{9,8},{10,11... | collective-permute-start | bytes 1179656 | tf_op jit(solution)/shard_map/ppermute | solution.py:453
  98.0 1.8 %collective-permute-start.6 = (bf16[48,32,128]{2,1,0:T(8,128)(2,1)S(1)}, bf16[48,32,128]{2,1,0:T(8,128)(2,1)S(1)}, u32[]{:S(2)}, u32[]{:S(2)}) collective-permute-start(bf16[48,32,128]{2,1,0:T(8,128)(2,1)S(1)} %get-tuple-element.45), channel_id=1, source_target_pairs={{0,1},{1,0},{2,3},{3,2},{4,5},{5,4},{6,7},{7,6},{8,9},{9,8},{10,11... | collective-permute-start | bytes 1179656 | tf_op jit(solution)/shard_map/ppermute | solution.py:453
  100.5 16.8 %collective-permute-start.7 = (bf16[192,32,128]{2,1,0:T(8,128)(2,1)S(1)}, bf16[192,32,128]{2,1,0:T(8,128)(2,1)S(1)}, u32[]{:S(2)}, u32[]{:S(2)}) collective-permute-start(bf16[192,32,128]{2,1,0:T(8,128)(2,1)S(1)} %get-tuple-element.49), channel_id=1, source_target_pairs={{0,1},{1,0},{2,3},{3,2},{4,5},{5,4},{6,7},{7,6},{8,9},{9,8},{10,11... | collective-permute-start | bytes 4718600 | tf_op jit(solution)/shard_map/ppermute | solution.py:453

commit v4 on v3

--- a/solution.py
+++ b/solution.py
@@ -57,20 +57,35 @@
     return total
 
 
-def first_payload_kernel(rhs_ref, send_ref, payload_ref):
+def first_payload_kernel(rhs_ref, send_ref, payload_ref, held, sems, listed, listed_sem):
     faces, rows, _ = rhs_ref.shape
+    parts = sems.shape[0]
+    count = faces // parts
+
+    def copy(part):
+        span = pl.ds(part * count, count)
+        return pltpu.make_async_copy(rhs_ref.at[span], held.at[span], sems.at[part])
+
+    for part in range(parts):
+        copy(part).start()
+    list_copy = pltpu.make_async_copy(send_ref, listed, listed_sem)
+    list_copy.start()
 
     def add(face, total):
-        value = rhs_ref[face].astype(f32)
+        value = held[face].astype(f32)
         return total + value * value
 
-    total = lax.fori_loop(0, faces, add, jnp.zeros((rows, P_SIZE), f32), unroll=8)
+    total = jnp.zeros((rows, P_SIZE), f32)
+    for part in range(parts):
+        copy(part).wait()
+        total = lax.fori_loop(part * count, (part + 1) * count, add, total, unroll=8)
     stats = stat_lanes([jnp.sum(total, axis=1, keepdims=True)]).astype(bf16)
+    list_copy.wait()
 
     @pl.loop(0, payload_ref.shape[0], unroll=4)
     def _(slot):
         payload_ref[slot] = stats
-        payload_ref[slot, :, :P_SIZE] = rhs_ref[send_ref[0, slot]]
+        payload_ref[slot, :, :P_SIZE] = held[listed[0, slot]]
 
 
 def relayout(source, perm_ref, tail_ref, target):
@@ -458,7 +473,15 @@
     rhs_other = swap(rhs)
 
     ghost_field = out((ghosts, half, LANES))
-    payload = call(first_payload_kernel, ghost_field, [VMEM, SMEM], limit=limit(4))(rhs, send_faces)
+    arriving = 4 if owned % 4 == 0 else 1
+    payload = call(
+        first_payload_kernel, ghost_field, [HBM, HBM],
+        [
+            pltpu.VMEM((owned, half, P_SIZE), bf16), pltpu.SemaphoreType.DMA((arriving,)),
+            pltpu.SMEM(send_faces.shape, jnp.int32), pltpu.SemaphoreType.DMA,
+        ],
+        limit=limit(4),
+    )(pltpu.with_memory_space_constraint(rhs, pltpu.HBM), pltpu.with_memory_space_constraint(send_faces, pltpu.HBM))
     ghost = exchange(payload)
 
     row = jnp.arange(group * group)

time: 121 us -> 120 us (level)
  local copies, waits for them, and re-layouts: 6.49 us -> 4.42 us
    unnamed x22 -> x18, local copies, waits for them, and re-layouts: 6.49 us -> 4.42 us
where the time goes in v4:
time: 120 us
  blocking collectives  71 us (59%)
  Pallas kernels  35.4 us (30%)
  waiting for transfers between devices  6.49 us (5%)
  local copies, waits for them, and re-layouts  4.42 us (4%)
  starting transfers between devices  1.31 us (1%)
    all_to_all x4, blocking collectives, exchange(): return lax.all_to_all(value, 'dom', split_axis=0, concat_axis=0, tiled=True)  71 us
    pallas_call x1, Pallas kernels, body(): call(functools.partial(first_apply_kernel, ranks, entries, resident), out...  16.6 us
    pallas_call x1, Pallas kernels, body(): call(functools.partial(second_apply_kernel, ranks, entries, resident), ou...  9.24 us
    ppermute x8, waiting for transfers between devices, swap(): return lax.ppermute(value, 'col', [(0, 1), (1, 0)])  6.49 us
    unnamed x18, local copies, waits for them, and re-layouts  4.42 us
    pallas_call x1, Pallas kernels, body(): call(functools.partial(final_kernel, ranks, entries), (jax.ShapeDtypeStru...  3.75 us
    pallas_call x1, Pallas kernels, body(): call(functools.partial(project_kernel, ranks, entries), (field, ghost_fie...  2.57 us
  transfers between devices with their start and end apart: 8, of which 4 were waited for; matrix products, arithmetic and copies ran while one was open for 0% of the time, Pallas kernels for 1%

profile of v4, /device:TPU:0, one launch (start us, length us, event | category | flops | bytes accessed | tf_op | source)
XLA Modules:
  0.0 119.6 jit_solution(9244020937170402336)
XLA Ops:
  0.6 0.5 collective-permute-start
  1.2 1.7 %shard_map.67 = bf16[48,32,128]{2,1,0:T(8,128)(2,1)S(1)} custom-call(bf16[192,32,105]{2,1,0:T(8,128)(2,1)} %bitcast.11, s32[1,48]{1,0:T(1,128)} %send_ref.5), custom_call_target="tpu_custom_call" | custom-call | tf_op jit(solution)/shard_map/pallas_call | solution.py:477
  2.9 20.9 %all_to_all.20.ghost_ref = bf16[48,32,128]{2,1,0:T(8,128)(2,1)S(1)} all-to-all(bf16[48,32,128]{2,1,0:T(8,128)(2,1)S(1)} %shard_map.67), channel_id=1, replica_groups=mesh['dom'=16,'col'=2] {'dom'}, dimensions={0} | all-to-all | bytes 786432 | tf_op jit(solution)/shard_map/all_to_all | solution.py:471
  23.8 0.0 collective-permute-start.1
  23.8 0.1 and_convert_fusion.refs_1_
  24.0 1.6 %collective-permute-done.1.ghost_other_ref = bf16[48,32,128]{2,1,0:T(8,128)(2,1)S(1)} collective-permute-done((bf16[48,32,128]{2,1,0:T(8,128)(2,1)S(1)}, bf16[48,32,128]{2,1,0:T(8,128)(2,1)S(1)}, u32[]{:S(2)}, u32[]{:S(2)}) %collective-permute-start.1) | collective-permute-done | bytes 393248 | tf_op jit(solution)/shard_map/ppermute | solution.py:468
  25.5 0.0 collective-permute-done.rhs_other_ref
  25.6 16.6 %shard_map.68 = (bf16[240,64,128]{2,1,0:T(8,128)(2,1)S(1)}, f32[240,64,128]{2,1,0:T(8,128)S(1)}, bf16[48,32,128]{2,1,0:T(8,128)(2,1)S(1)}, bf16[48,32,128]{2,1,0...) custom-call(bf16[192,32,105]{2,1,0:T(8,128)(2,1)S(1)} %bitcast.12, ...), custom_call_target="tpu_custom_call" | custom-call | tf_op jit(solution)/shard_map/pallas_call | solution.py:515
  42.2 3.2 %copy-done.1 = bf16[32,256,512]{2,1,0:T(8,128)(2,1)} copy-done((bf16[32,256,512]{2,1,0:T(8,128)(2,1)}, bf16[32,256,512]{2,1,0:T(8,128)(2,1)S(1)}, u32[]{:S(2)}) %copy-start.1) | copy-done | bytes 8388632
  45.4 0.1 collective-permute-start.2
  45.5 1.6 %collective-permute-done.2.other_ref = bf16[48,32,128]{2,1,0:T(8,128)(2,1)S(1)} collective-permute-done((bf16[48,32,128]{2,1,0:T(8,128)(2,1)S(1)}, bf16[48,32,128]{2,1,0:T(8,128)(2,1)S(1)}, u32[]{:S(2)}, u32[]{:S(2)}) %collective-permute-start.2) | collective-permute-done | bytes 393248 | tf_op jit(solution)/shard_map/ppermute | solution.py:468
  47.1 0.4 shard_map.69
  47.6 1.2 copy-done
  48.8 0.4 shard_map.70
  49.2 0.2 collective-permute-start.3
  49.4 16.9 %all_to_all.21.returned_ref = bf16[48,32,128]{2,1,0:T(8,128)(2,1)S(1)} all-to-all(bf16[48,32,128]{2,1,0:T(8,128)(2,1)S(1)} %get-tuple-element.36), channel_id=1, replica_groups=mesh['dom'=16,'col'=2] {'dom'}, dimensions={0} | all-to-all | bytes 786432 | tf_op jit(solution)/shard_map/all_to_all | solution.py:471
  66.2 0.0 collective-permute-done.3.other_ref
  66.2 2.6 %shard_map.71 = (bf16[192,32,128]{2,1,0:T(8,128)(2,1)S(1)}, bf16[48,32,128]{2,1,0:T(8,128)(2,1)S(1)}, f32[32,128]{1,0:T(8,128)S(1)}) custom-call(bf16[192,32,128]{2,1,0:T(8,128)(2,1)S(1)} %get-tuple-element.34.own_ref, bf16[192,32,128]{2,1,0:T(8,128)(2,1)S(1)} %collective-permute-done.3.other_ref, bf16[48,32,128]{2,1,0:T(8,128)(2,1)S(1)} %all_to_all.21.returned_ref, ...), custom_call_target="tpu_custom_call" | custom-call | tf_op jit(solution)/shard_map/pallas_call | solution.py:535
  68.8 0.1 collective-permute-start.4
  68.9 16.6 %all_to_all.22.ghost_ref = bf16[48,32,128]{2,1,0:T(8,128)(2,1)S(1)} all-to-all(bf16[48,32,128]{2,1,0:T(8,128)(2,1)S(1)} %get-tuple-element.39), channel_id=1, replica_groups=mesh['dom'=16,'col'=2] {'dom'}, dimensions={0} | all-to-all | bytes 786432 | tf_op jit(solution)/shard_map/all_to_all | solution.py:471
  85.5 0.0 collective-permute-start.5
  85.5 1.7 %collective-permute-done.5.ghost_other_ref = bf16[48,32,128]{2,1,0:T(8,128)(2,1)S(1)} collective-permute-done((bf16[48,32,128]{2,1,0:T(8,128)(2,1)S(1)}, bf16[48,32,128]{2,1,0:T(8,128)(2,1)S(1)}, u32[]{:S(2)}, u32[]{:S(2)}) %collective-permute-start.5) | collective-permute-done | bytes 393248 | tf_op jit(solution)/shard_map/ppermute | solution.py:468
  87.2 0.0 collective-permute-done.4.rounded_other_ref
  87.3 9.2 %shard_map.72 = (bf16[240,64,128]{2,1,0:T(8,128)(2,1)S(1)}, f32[240,64,128]{2,1,0:T(8,128)S(1)}, bf16[48,32,128]{2,1,0:T(8,128)(2,1)S(1)}, bf16[48,32,128]{2,1,0...) custom-call(bf16[192,32,128]{2,1,0:T(8,128)(2,1)S(1)} %get-tuple-element, ...), custom_call_target="tpu_custom_call", output_to_operand_aliasing={{1}: (6, {})} | custom-call | tf_op jit(solution)/shard_map/pallas_call | solution.py:546
  96.5 0.2 collective-permute-start.6
  96.7 1.6 %collective-permute-done.6.other_ref = bf16[48,32,128]{2,1,0:T(8,128)(2,1)S(1)} collective-permute-done((bf16[48,32,128]{2,1,0:T(8,128)(2,1)S(1)}, bf16[48,32,128]{2,1,0:T(8,128)(2,1)S(1)}, u32[]{:S(2)}, u32[]{:S(2)}) %collective-permute-start.6) | collective-permute-done | bytes 393248 | tf_op jit(solution)/shard_map/ppermute | solution.py:468
  98.3 0.3 shard_map.73
  98.6 0.4 shard_map.74
  99.0 0.2 collective-permute-start.7
  99.2 16.6 %all_to_all.23.returned_ref = bf16[48,32,128]{2,1,0:T(8,128)(2,1)S(1)} all-to-all(bf16[48,32,128]{2,1,0:T(8,128)(2,1)S(1)} %get-tuple-element.50), channel_id=1, replica_groups=mesh['dom'=16,'col'=2] {'dom'}, dimensions={0} | all-to-all | bytes 786432 | tf_op jit(solution)/shard_map/all_to_all | solution.py:471
  115.8 0.0 collective-permute-done.7.other_ref
  115.8 3.8 %shard_map.75 = (bf16[192,32,105]{2,1,0:T(8,128)(2,1)}, f32[5,32]{1,0:T(8,128)}) custom-call(bf16[192,32,128]{2,1,0:T(8,128)(2,1)S(1)} %get-tuple-element.48.own_ref, bf16[192,32,128]{2,1,0:T(8,128)(2,1)S(1)} %collective-permute-done.7.other_ref, bf16[48,32,128]{2,1,0:T(8,128)(2,1)S(1)} %all_to_all.23.returned_ref, ...), custom_call_target="tpu_custom_call" | custom-call | tf_op jit(solution)/shard_map/pallas_call | solution.py:561
  (19 shorter events, 0.0 us)
Async XLA Ops:
  0.6 24.9 %copy-start.2 = (bf16[192,105,32]{1,2,0:T(8,128)(2,1)S(1)}, bf16[192,105,32]{1,2,0:T(8,128)(2,1)}, u32[]{:S(2)}) copy-start(bf16[192,105,32]{1,2,0:T(8,128)(2,1)} %param.4) | copy-start | bytes 3870724
  0.6 24.9 %copy-start.3 = (s32[96,4]{0,1:T(4,128)S(1)}, s32[96,4]{0,1:T(4,128)}, u32[]{:S(2)}) copy-start(s32[96,4]{0,1:T(4,128)} %param.6) | copy-start | bytes 4612
  0.6 24.9 %collective-permute-start = (bf16[192,32,105]{2,1,0:T(8,128)(2,1)}, bf16[192,32,105]{2,1,0:T(8,128)(2,1)S(1)}, u32[]{:S(2)}, u32[]{:S(2)}) collective-permute-start(bf16[192,32,105]{2,1,0:T(8,128)(2,1)} %bitcast.10), channel_id=1, source_target_pairs={{0,1},{1,0},{2,3},{3,2},{4,5},{5,4},{6,7},{7,6},{8,9},{9,8},{10,11... | collective-permute-start | bytes 3870728 | tf_op jit(solution)/shard_map/ppermute | solution.py:468
  23.8 1.7 %collective-permute-start.1 = (bf16[48,32,128]{2,1,0:T(8,128)(2,1)S(1)}, bf16[48,32,128]{2,1,0:T(8,128)(2,1)S(1)}, u32[]{:S(2)}, u32[]{:S(2)}) collective-permute-start(bf16[48,32,128]{2,1,0:T(8,128)(2,1)S(1)} %all_to_all.20.ghost_ref), channel_id=1, source_target_pairs={{0,1},{1,0},{2,3},{3,2},{4,5},{5,4},{6,7},{7,6},{8,9},{9,8},{10,11... | collective-permute-start | bytes 1179656 | tf_op jit(solution)/shard_map/ppermute | solution.py:468
  42.2 3.2 %copy-start.1 = (bf16[32,256,512]{2,1,0:T(8,128)(2,1)}, bf16[32,256,512]{2,1,0:T(8,128)(2,1)S(1)}, u32[]{:S(2)}) copy-start(bf16[32,256,512]{2,1,0:T(8,128)(2,1)S(1)} %get-tuple-element.42.refs_2_) | copy-start | bytes 25165828
  45.4 3.4 %copy-start = (bf16[32,256,512]{2,1,0:T(8,128)(2,1)}, bf16[32,256,512]{2,1,0:T(8,128)(2,1)S(1)}, u32[]{:S(2)}) copy-start(bf16[32,256,512]{2,1,0:T(8,128)(2,1)S(1)} %get-tuple-element.41.refs_1_) | copy-start | bytes 25165828
  45.4 1.7 %collective-permute-start.2 = (bf16[48,32,128]{2,1,0:T(8,128)(2,1)S(1)}, bf16[48,32,128]{2,1,0:T(8,128)(2,1)S(1)}, u32[]{:S(2)}, u32[]{:S(2)}) collective-permute-start(bf16[48,32,128]{2,1,0:T(8,128)(2,1)S(1)} %get-tuple-element.31), channel_id=1, source_target_pairs={{0,1},{1,0},{2,3},{3,2},{4,5},{5,4},{6,7},{7,6},{8,9},{9,8},{10,11... | collective-permute-start | bytes 1179656 | tf_op jit(solution)/shard_map/ppermute | solution.py:468
  47.1 40.1 %slice-start.2 = ((s8[8388608]{0:T(1024)(128)(4,1)}), s8[4194304]{0:T(1024)(128)(4,1)S(1)}, s32[]{:S(2)}) async-start(s8[8388608]{0:T(1024)(128)(4,1)} %bitcast.8), calls=%async_computation.6 | async-start | bytes 8388608
  48.8 17.5 %copy-start.4 = (s32[1,48]{1,0:T(1,128)S(1)}, s32[1,48]{1,0:T(1,128)}, u32[]{:S(2)}) copy-start(s32[1,48]{1,0:T(1,128)} %send_ref.5) | copy-start | bytes 580
  48.8 38.5 %slice-start = ((s8[8388608]{0:T(1024)(128)(4,1)}), s8[4194304]{0:T(1024)(128)(4,1)S(1)}, s32[]{:S(2)}) async-start(s8[8388608]{0:T(1024)(128)(4,1)} %bitcast.6), calls=%async_computation.4 | async-start | bytes 8388608
  48.8 38.5 %slice-start.3 = ((s8[8388608]{0:T(1024)(128)(4,1)}), s8[4194304]{0:T(1024)(128)(4,1)S(1)}, s32[]{:S(2)}) async-start(s8[8388608]{0:T(1024)(128)(4,1)} %bitcast.8), calls=%async_computation.7 | async-start | bytes 8388608
  49.2 17.0 %collective-permute-start.3 = (bf16[192,32,128]{2,1,0:T(8,128)(2,1)S(1)}, bf16[192,32,128]{2,1,0:T(8,128)(2,1)S(1)}, u32[]{:S(2)}, u32[]{:S(2)}) collective-permute-start(bf16[192,32,128]{2,1,0:T(8,128)(2,1)S(1)} %get-tuple-element.35), channel_id=1, source_target_pairs={{0,1},{1,0},{2,3},{3,2},{4,5},{5,4},{6,7},{7,6},{8,9},{9,8},{10,11... | collective-permute-start | bytes 4718600 | tf_op jit(solution)/shard_map/ppermute | solution.py:468
  49.4 37.9 %slice-start.1 = ((s8[8388608]{0:T(1024)(128)(4,1)}), s8[4194304]{0:T(1024)(128)(4,1)S(1)}, s32[]{:S(2)}) async-start(s8[8388608]{0:T(1024)(128)(4,1)} %bitcast.6), calls=%async_computation.5 | async-start | bytes 8388608
  68.8 18.4 %collective-permute-start.4 = (bf16[192,32,128]{2,1,0:T(8,128)(2,1)S(1)}, bf16[192,32,128]{2,1,0:T(8,128)(2,1)S(1)}, u32[]{:S(2)}, u32[]{:S(2)}) collective-permute-start(bf16[192,32,128]{2,1,0:T(8,128)(2,1)S(1)} %get-tuple-element.38.rounded_ref), channel_id=1, source_target_pairs={{0,1},{1,0},{2,3},{3,2},{4,5},{5,4},{6,7},{7,6},{8,9},{9,8},{10,11... | collective-permute-start | bytes 4718600 | tf_op jit(solution)/shard_map/ppermute | solution.py:468
  85.5 1.7 %collective-permute-start.5 = (bf16[48,32,128]{2,1,0:T(8,128)(2,1)S(1)}, bf16[48,32,128]{2,1,0:T(8,128)(2,1)S(1)}, u32[]{:S(2)}, u32[]{:S(2)}) collective-permute-start(bf16[48,32,128]{2,1,0:T(8,128)(2,1)S(1)} %all_to_all.22.ghost_ref), channel_id=1, source_target_pairs={{0,1},{1,0},{2,3},{3,2},{4,5},{5,4},{6,7},{7,6},{8,9},{9,8},{10,11... | collective-permute-start | bytes 1179656 | tf_op jit(solution)/shard_map/ppermute | solution.py:468
  96.5 1.8 %collective-permute-start.6 = (bf16[48,32,128]{2,1,0:T(8,128)(2,1)S(1)}, bf16[48,32,128]{2,1,0:T(8,128)(2,1)S(1)}, u32[]{:S(2)}, u32[]{:S(2)}) collective-permute-start(bf16[48,32,128]{2,1,0:T(8,128)(2,1)S(1)} %get-tuple-element.45), channel_id=1, source_target_pairs={{0,1},{1,0},{2,3},{3,2},{4,5},{5,4},{6,7},{7,6},{8,9},{9,8},{10,11... | collective-permute-start | bytes 1179656 | tf_op jit(solution)/shard_map/ppermute | solution.py:468
  99.0 16.8 %collective-permute-start.7 = (bf16[192,32,128]{2,1,0:T(8,128)(2,1)S(1)}, bf16[192,32,128]{2,1,0:T(8,128)(2,1)S(1)}, u32[]{:S(2)}, u32[]{:S(2)}) collective-permute-start(bf16[192,32,128]{2,1,0:T(8,128)(2,1)S(1)} %get-tuple-element.49), channel_id=1, source_target_pairs={{0,1},{1,0},{2,3},{3,2},{4,5},{5,4},{6,7},{7,6},{8,9},{9,8},{10,11... | collective-permute-start | bytes 4718600 | tf_op jit(solution)/shard_map/ppermute | solution.py:468

commit v5 on v4

--- a/solution.py
+++ b/solution.py
@@ -273,9 +273,11 @@
     @pl.loop(0, owned, unroll=4)
     def _(face):
         sums_ref[face] = jnp.zeros((rows, LANES), f32)
-        basis_ref[face] = jnp.zeros((rows, LANES), bf16)
-        basis_ref[face, :half, :P_SIZE] = (rhs_ref[face].astype(f32) * scale).astype(bf16)
-        basis_ref[face, half:, :P_SIZE] = (rhs_other_ref[face].astype(f32) * scale_other).astype(bf16)
+        spare = jnp.zeros((half, LANES - P_SIZE), f32)
+        own = jnp.concatenate([rhs_ref[face].astype(f32) * scale, spare], axis=1)
+        other = jnp.concatenate([rhs_other_ref[face].astype(f32) * scale_other, spare], axis=1)
+        basis_ref[face, :half] = own.astype(bf16)
+        basis_ref[face, half:] = other.astype(bf16)
 
     fill_ghosts(basis_ref, sums_ref, ghost_ref, ghost_other_ref, scale, scale_other)
     field = (basis_ref, faces_ref, 2 * lax.axis_index("col"), sums_ref)
@@ -333,7 +335,7 @@
             - diagonal * basis_ref[face, :half].astype(f32)
         )
 
-    @pl.loop(0, ghosts)
+    @pl.loop(0, ghosts, unroll=8)
     def _(slot):
         projected_ref[send_ref[0, slot]] += returned_ref[slot].astype(f32)
 
@@ -411,7 +413,7 @@
         )
         image_ref[face] = value - proj_second * second_ref[face, :half].astype(f32)
 
-    @pl.loop(0, returned_ref.shape[0])
+    @pl.loop(0, returned_ref.shape[0], unroll=8)
     def _(slot):
         image_ref[send_ref[0, slot]] += returned_ref[slot].astype(f32)
 

time: 120 us -> 120 us (level)
  no operation moved by 1% of the time
where the time goes in v5:
time: 120 us; the launch traced here: 119 us
  blocking collectives  71 us (59%)
  Pallas kernels  35.1 us (29%)
  waiting for transfers between devices  6.49 us (5%)
  local copies, waits for them, and re-layouts  4.42 us (4%)
  starting transfers between devices  1.31 us (1%)
    all_to_all x4, blocking collectives, exchange(): return lax.all_to_all(value, 'dom', split_axis=0, concat_axis=0, tiled=True)  71 us
    pallas_call x1, Pallas kernels, body(): call(functools.partial(first_apply_kernel, ranks, entries, resident), out...  16.6 us
    pallas_call x1, Pallas kernels, body(): call(functools.partial(second_apply_kernel, ranks, entries, resident), ou...  9.24 us
    ppermute x8, waiting for transfers between devices, swap(): return lax.ppermute(value, 'col', [(0, 1), (1, 0)])  6.49 us
    unnamed x18, local copies, waits for them, and re-layouts  4.42 us
    pallas_call x1, Pallas kernels, body(): call(functools.partial(final_kernel, ranks, entries), (jax.ShapeDtypeStru...  3.6 us
    pallas_call x1, Pallas kernels, body(): call(functools.partial(project_kernel, ranks, entries), (field, ghost_fie...  2.42 us
  transfers between devices with their start and end apart: 8, of which 4 were waited for; matrix products, arithmetic and copies ran while one was open for 0% of the time, Pallas kernels for 1%

profile of v5, /device:TPU:0, one launch (start us, length us, event | category | flops | bytes accessed | tf_op | source)
XLA Modules:
  0.0 119.3 jit_solution(11850239436403090700)
XLA Ops:
  0.6 0.5 collective-permute-start
  1.2 1.7 %shard_map.67 = bf16[48,32,128]{2,1,0:T(8,128)(2,1)S(1)} custom-call(bf16[192,32,105]{2,1,0:T(8,128)(2,1)} %bitcast.11, s32[1,48]{1,0:T(1,128)} %send_ref.5), custom_call_target="tpu_custom_call" | custom-call | tf_op jit(solution)/shard_map/pallas_call | solution.py:479
  2.9 20.9 %all_to_all.20.ghost_ref = bf16[48,32,128]{2,1,0:T(8,128)(2,1)S(1)} all-to-all(bf16[48,32,128]{2,1,0:T(8,128)(2,1)S(1)} %shard_map.67), channel_id=1, replica_groups=mesh['dom'=16,'col'=2] {'dom'}, dimensions={0} | all-to-all | bytes 786432 | tf_op jit(solution)/shard_map/all_to_all | solution.py:473
  23.8 0.0 collective-permute-start.1
  23.8 0.1 and_convert_fusion.refs_1_
  24.0 1.6 %collective-permute-done.1.ghost_other_ref = bf16[48,32,128]{2,1,0:T(8,128)(2,1)S(1)} collective-permute-done((bf16[48,32,128]{2,1,0:T(8,128)(2,1)S(1)}, bf16[48,32,128]{2,1,0:T(8,128)(2,1)S(1)}, u32[]{:S(2)}, u32[]{:S(2)}) %collective-permute-start.1) | collective-permute-done | bytes 393248 | tf_op jit(solution)/shard_map/ppermute | solution.py:470
  25.5 0.0 collective-permute-done.rhs_other_ref
  25.6 16.6 %shard_map.68 = (bf16[240,64,128]{2,1,0:T(8,128)(2,1)S(1)}, f32[240,64,128]{2,1,0:T(8,128)S(1)}, bf16[48,32,128]{2,1,0:T(8,128)(2,1)S(1)}, bf16[48,32,128]{2,1,0...) custom-call(bf16[192,32,105]{2,1,0:T(8,128)(2,1)S(1)} %bitcast.12, ...), custom_call_target="tpu_custom_call" | custom-call | tf_op jit(solution)/shard_map/pallas_call | solution.py:517
  42.2 3.2 %copy-done.1 = bf16[32,256,512]{2,1,0:T(8,128)(2,1)} copy-done((bf16[32,256,512]{2,1,0:T(8,128)(2,1)}, bf16[32,256,512]{2,1,0:T(8,128)(2,1)S(1)}, u32[]{:S(2)}) %copy-start.1) | copy-done | bytes 8388632
  45.4 0.1 collective-permute-start.2
  45.5 1.6 %collective-permute-done.2.other_ref = bf16[48,32,128]{2,1,0:T(8,128)(2,1)S(1)} collective-permute-done((bf16[48,32,128]{2,1,0:T(8,128)(2,1)S(1)}, bf16[48,32,128]{2,1,0:T(8,128)(2,1)S(1)}, u32[]{:S(2)}, u32[]{:S(2)}) %collective-permute-start.2) | collective-permute-done | bytes 393248 | tf_op jit(solution)/shard_map/ppermute | solution.py:470
  47.1 0.4 shard_map.69
  47.6 1.2 copy-done
  48.8 0.4 shard_map.70
  49.2 0.2 collective-permute-start.3
  49.4 16.9 %all_to_all.21.returned_ref = bf16[48,32,128]{2,1,0:T(8,128)(2,1)S(1)} all-to-all(bf16[48,32,128]{2,1,0:T(8,128)(2,1)S(1)} %get-tuple-element.36), channel_id=1, replica_groups=mesh['dom'=16,'col'=2] {'dom'}, dimensions={0} | all-to-all | bytes 786432 | tf_op jit(solution)/shard_map/all_to_all | solution.py:473
  66.2 0.0 collective-permute-done.3.other_ref
  66.2 2.4 %shard_map.71 = (bf16[192,32,128]{2,1,0:T(8,128)(2,1)S(1)}, bf16[48,32,128]{2,1,0:T(8,128)(2,1)S(1)}, f32[32,128]{1,0:T(8,128)S(1)}) custom-call(bf16[192,32,128]{2,1,0:T(8,128)(2,1)S(1)} %get-tuple-element.34.own_ref, bf16[192,32,128]{2,1,0:T(8,128)(2,1)S(1)} %collective-permute-done.3.other_ref, bf16[48,32,128]{2,1,0:T(8,128)(2,1)S(1)} %all_to_all.21.returned_ref, ...), custom_call_target="tpu_custom_call" | custom-call | tf_op jit(solution)/shard_map/pallas_call | solution.py:537
  68.7 0.1 collective-permute-start.4
  68.7 16.6 %all_to_all.22.ghost_ref = bf16[48,32,128]{2,1,0:T(8,128)(2,1)S(1)} all-to-all(bf16[48,32,128]{2,1,0:T(8,128)(2,1)S(1)} %get-tuple-element.39), channel_id=1, replica_groups=mesh['dom'=16,'col'=2] {'dom'}, dimensions={0} | all-to-all | bytes 786432 | tf_op jit(solution)/shard_map/all_to_all | solution.py:473
  85.4 0.0 collective-permute-start.5
  85.4 1.7 %collective-permute-done.5.ghost_other_ref = bf16[48,32,128]{2,1,0:T(8,128)(2,1)S(1)} collective-permute-done((bf16[48,32,128]{2,1,0:T(8,128)(2,1)S(1)}, bf16[48,32,128]{2,1,0:T(8,128)(2,1)S(1)}, u32[]{:S(2)}, u32[]{:S(2)}) %collective-permute-start.5) | collective-permute-done | bytes 393248 | tf_op jit(solution)/shard_map/ppermute | solution.py:470
  87.1 0.0 collective-permute-done.4.rounded_other_ref
  87.1 9.2 %shard_map.72 = (bf16[240,64,128]{2,1,0:T(8,128)(2,1)S(1)}, f32[240,64,128]{2,1,0:T(8,128)S(1)}, bf16[48,32,128]{2,1,0:T(8,128)(2,1)S(1)}, bf16[48,32,128]{2,1,0...) custom-call(bf16[192,32,128]{2,1,0:T(8,128)(2,1)S(1)} %get-tuple-element, ...), custom_call_target="tpu_custom_call", output_to_operand_aliasing={{1}: (6, {})} | custom-call | tf_op jit(solution)/shard_map/pallas_call | solution.py:548
  96.4 0.2 collective-permute-start.6
  96.6 1.6 %collective-permute-done.6.other_ref = bf16[48,32,128]{2,1,0:T(8,128)(2,1)S(1)} collective-permute-done((bf16[48,32,128]{2,1,0:T(8,128)(2,1)S(1)}, bf16[48,32,128]{2,1,0:T(8,128)(2,1)S(1)}, u32[]{:S(2)}, u32[]{:S(2)}) %collective-permute-start.6) | collective-permute-done | bytes 393248 | tf_op jit(solution)/shard_map/ppermute | solution.py:470
  98.2 0.3 shard_map.73
  98.4 0.4 shard_map.74
  98.9 0.2 collective-permute-start.7
  99.1 16.6 %all_to_all.23.returned_ref = bf16[48,32,128]{2,1,0:T(8,128)(2,1)S(1)} all-to-all(bf16[48,32,128]{2,1,0:T(8,128)(2,1)S(1)} %get-tuple-element.50), channel_id=1, replica_groups=mesh['dom'=16,'col'=2] {'dom'}, dimensions={0} | all-to-all | bytes 786432 | tf_op jit(solution)/shard_map/all_to_all | solution.py:473
  115.7 0.0 collective-permute-done.7.other_ref
  115.7 3.6 %shard_map.75 = (bf16[192,32,105]{2,1,0:T(8,128)(2,1)}, f32[5,32]{1,0:T(8,128)}) custom-call(bf16[192,32,128]{2,1,0:T(8,128)(2,1)S(1)} %get-tuple-element.48.own_ref, bf16[192,32,128]{2,1,0:T(8,128)(2,1)S(1)} %collective-permute-done.7.other_ref, bf16[48,32,128]{2,1,0:T(8,128)(2,1)S(1)} %all_to_all.23.returned_ref, ...), custom_call_target="tpu_custom_call" | custom-call | tf_op jit(solution)/shard_map/pallas_call | solution.py:563
  (19 shorter events, 0.0 us)
Async XLA Ops:
  0.6 24.9 %copy-start.2 = (bf16[192,105,32]{1,2,0:T(8,128)(2,1)S(1)}, bf16[192,105,32]{1,2,0:T(8,128)(2,1)}, u32[]{:S(2)}) copy-start(bf16[192,105,32]{1,2,0:T(8,128)(2,1)} %param.4) | copy-start | bytes 3870724
  0.6 24.9 %copy-start.3 = (s32[96,4]{0,1:T(4,128)S(1)}, s32[96,4]{0,1:T(4,128)}, u32[]{:S(2)}) copy-start(s32[96,4]{0,1:T(4,128)} %param.6) | copy-start | bytes 4612
  0.6 24.9 %collective-permute-start = (bf16[192,32,105]{2,1,0:T(8,128)(2,1)}, bf16[192,32,105]{2,1,0:T(8,128)(2,1)S(1)}, u32[]{:S(2)}, u32[]{:S(2)}) collective-permute-start(bf16[192,32,105]{2,1,0:T(8,128)(2,1)} %bitcast.10), channel_id=1, source_target_pairs={{0,1},{1,0},{2,3},{3,2},{4,5},{5,4},{6,7},{7,6},{8,9},{9,8},{10,11... | collective-permute-start | bytes 3870728 | tf_op jit(solution)/shard_map/ppermute | solution.py:470
  23.8 1.7 %collective-permute-start.1 = (bf16[48,32,128]{2,1,0:T(8,128)(2,1)S(1)}, bf16[48,32,128]{2,1,0:T(8,128)(2,1)S(1)}, u32[]{:S(2)}, u32[]{:S(2)}) collective-permute-start(bf16[48,32,128]{2,1,0:T(8,128)(2,1)S(1)} %all_to_all.20.ghost_ref), channel_id=1, source_target_pairs={{0,1},{1,0},{2,3},{3,2},{4,5},{5,4},{6,7},{7,6},{8,9},{9,8},{10,11... | collective-permute-start | bytes 1179656 | tf_op jit(solution)/shard_map/ppermute | solution.py:470
  42.2 3.2 %copy-start.1 = (bf16[32,256,512]{2,1,0:T(8,128)(2,1)}, bf16[32,256,512]{2,1,0:T(8,128)(2,1)S(1)}, u32[]{:S(2)}) copy-start(bf16[32,256,512]{2,1,0:T(8,128)(2,1)S(1)} %get-tuple-element.42.refs_2_) | copy-start | bytes 25165828
  45.4 3.4 %copy-start = (bf16[32,256,512]{2,1,0:T(8,128)(2,1)}, bf16[32,256,512]{2,1,0:T(8,128)(2,1)S(1)}, u32[]{:S(2)}) copy-start(bf16[32,256,512]{2,1,0:T(8,128)(2,1)S(1)} %get-tuple-element.41.refs_1_) | copy-start | bytes 25165828
  45.4 1.7 %collective-permute-start.2 = (bf16[48,32,128]{2,1,0:T(8,128)(2,1)S(1)}, bf16[48,32,128]{2,1,0:T(8,128)(2,1)S(1)}, u32[]{:S(2)}, u32[]{:S(2)}) collective-permute-start(bf16[48,32,128]{2,1,0:T(8,128)(2,1)S(1)} %get-tuple-element.31), channel_id=1, source_target_pairs={{0,1},{1,0},{2,3},{3,2},{4,5},{5,4},{6,7},{7,6},{8,9},{9,8},{10,11... | collective-permute-start | bytes 1179656 | tf_op jit(solution)/shard_map/ppermute | solution.py:470
  47.1 40.0 %slice-start.2 = ((s8[8388608]{0:T(1024)(128)(4,1)}), s8[4194304]{0:T(1024)(128)(4,1)S(1)}, s32[]{:S(2)}) async-start(s8[8388608]{0:T(1024)(128)(4,1)} %bitcast.8), calls=%async_computation.6 | async-start | bytes 8388608
  48.8 17.5 %copy-start.4 = (s32[1,48]{1,0:T(1,128)S(1)}, s32[1,48]{1,0:T(1,128)}, u32[]{:S(2)}) copy-start(s32[1,48]{1,0:T(1,128)} %send_ref.5) | copy-start | bytes 580
  48.8 38.3 %slice-start = ((s8[8388608]{0:T(1024)(128)(4,1)}), s8[4194304]{0:T(1024)(128)(4,1)S(1)}, s32[]{:S(2)}) async-start(s8[8388608]{0:T(1024)(128)(4,1)} %bitcast.6), calls=%async_computation.4 | async-start | bytes 8388608
  48.8 38.3 %slice-start.3 = ((s8[8388608]{0:T(1024)(128)(4,1)}), s8[4194304]{0:T(1024)(128)(4,1)S(1)}, s32[]{:S(2)}) async-start(s8[8388608]{0:T(1024)(128)(4,1)} %bitcast.8), calls=%async_computation.7 | async-start | bytes 8388608
  49.2 17.1 %collective-permute-start.3 = (bf16[192,32,128]{2,1,0:T(8,128)(2,1)S(1)}, bf16[192,32,128]{2,1,0:T(8,128)(2,1)S(1)}, u32[]{:S(2)}, u32[]{:S(2)}) collective-permute-start(bf16[192,32,128]{2,1,0:T(8,128)(2,1)S(1)} %get-tuple-element.35), channel_id=1, source_target_pairs={{0,1},{1,0},{2,3},{3,2},{4,5},{5,4},{6,7},{7,6},{8,9},{9,8},{10,11... | collective-permute-start | bytes 4718600 | tf_op jit(solution)/shard_map/ppermute | solution.py:470
  49.4 37.7 %slice-start.1 = ((s8[8388608]{0:T(1024)(128)(4,1)}), s8[4194304]{0:T(1024)(128)(4,1)S(1)}, s32[]{:S(2)}) async-start(s8[8388608]{0:T(1024)(128)(4,1)} %bitcast.6), calls=%async_computation.5 | async-start | bytes 8388608
  68.7 18.4 %collective-permute-start.4 = (bf16[192,32,128]{2,1,0:T(8,128)(2,1)S(1)}, bf16[192,32,128]{2,1,0:T(8,128)(2,1)S(1)}, u32[]{:S(2)}, u32[]{:S(2)}) collective-permute-start(bf16[192,32,128]{2,1,0:T(8,128)(2,1)S(1)} %get-tuple-element.38.rounded_ref), channel_id=1, source_target_pairs={{0,1},{1,0},{2,3},{3,2},{4,5},{5,4},{6,7},{7,6},{8,9},{9,8},{10,11... | collective-permute-start | bytes 4718600 | tf_op jit(solution)/shard_map/ppermute | solution.py:470
  85.4 1.7 %collective-permute-start.5 = (bf16[48,32,128]{2,1,0:T(8,128)(2,1)S(1)}, bf16[48,32,128]{2,1,0:T(8,128)(2,1)S(1)}, u32[]{:S(2)}, u32[]{:S(2)}) collective-permute-start(bf16[48,32,128]{2,1,0:T(8,128)(2,1)S(1)} %all_to_all.22.ghost_ref), channel_id=1, source_target_pairs={{0,1},{1,0},{2,3},{3,2},{4,5},{5,4},{6,7},{7,6},{8,9},{9,8},{10,11... | collective-permute-start | bytes 1179656 | tf_op jit(solution)/shard_map/ppermute | solution.py:470
  96.4 1.8 %collective-permute-start.6 = (bf16[48,32,128]{2,1,0:T(8,128)(2,1)S(1)}, bf16[48,32,128]{2,1,0:T(8,128)(2,1)S(1)}, u32[]{:S(2)}, u32[]{:S(2)}) collective-permute-start(bf16[48,32,128]{2,1,0:T(8,128)(2,1)S(1)} %get-tuple-element.45), channel_id=1, source_target_pairs={{0,1},{1,0},{2,3},{3,2},{4,5},{5,4},{6,7},{7,6},{8,9},{9,8},{10,11... | collective-permute-start | bytes 1179656 | tf_op jit(solution)/shard_map/ppermute | solution.py:470
  98.9 16.8 %collective-permute-start.7 = (bf16[192,32,128]{2,1,0:T(8,128)(2,1)S(1)}, bf16[192,32,128]{2,1,0:T(8,128)(2,1)S(1)}, u32[]{:S(2)}, u32[]{:S(2)}) collective-permute-start(bf16[192,32,128]{2,1,0:T(8,128)(2,1)S(1)} %get-tuple-element.49), channel_id=1, source_target_pairs={{0,1},{1,0},{2,3},{3,2},{4,5},{5,4},{6,7},{7,6},{8,9},{9,8},{10,11... | collective-permute-start | bytes 4718600 | tf_op jit(solution)/shard_map/ppermute | solution.py:470
